TPU v7x, 32 devices: a whole 2x2x4 slice. The times are simulated.
32 devices in a mesh: group: 2 (over y), query: 4 (over x, core), memory: 4 (over z).
Axes of the slice: x: 2, y: 2, z: 4, core: 2. Of those that a mesh axis runs over, the one named last changes fastest.
Arguments:
- queries: bfloat16 [4096, 2048], P(('group', 'query', 'memory')), parts along dimension 0, may hold values from -140 to 140
- keys: bfloat16 [8192, 2048], P(('group', 'memory'), 'query'), parts along dimension 0, may hold values from -6.1 to 6.1
- values: bfloat16 [8192, 2048], P(('group', 'memory'), 'query'), parts along dimension 0, may hold values from -6 to 6
- grad_out: bfloat16 [4096, 2048], P(('group', 'query', 'memory')), parts along dimension 0, may hold values from -6 to 6
- blocks: int32 [16, 32, 2], P(None, 'group'), parts along dimension 1, may hold values from 0 to 31, as said below
Outputs:
- grad_q: bfloat16 [4096, 2048], P(('group', 'query', 'memory')), parts along dimension 0
- grad_k: bfloat16 [8192, 2048], P(('group', 'memory'), 'query'), parts along dimension 0
- grad_v: bfloat16 [8192, 2048], P(('group', 'memory'), 'query'), parts along dimension 0
There are 2 independent parts, one for each index of `group`. A program takes and returns all parts, laid end to end along the dimension named above; each array names one. Nothing has to cross between parts.
Inputs may be any that keep to these rules, and one draw needn't show every extreme that they name: blocks[h, b, 0] and blocks[h, b, 1] are two different memory blocks of 128 rows.
All inputs are finite; a program needn't handle non-finite values.
Results may differ from a plain program's by a relative error of at most 0.0056.
Values may be sent and summed in bfloat16 or wider, within the bound.
A program may use at most 128 MiB of HBM per device.

v0:
```python
import math

import jax
import jax.numpy as jnp
from jax import lax
from jax.sharding import PartitionSpec as P

HEAD_DIM = 128
BLOCK = 128


def joined(value, axis, combine):
    everything = jax.tree.map(lambda part: lax.all_gather(part, axis), value)
    leading = jax.tree.map(lambda part: part[0], everything)

    def hop(k, so_far):
        return combine(so_far, jax.tree.map(lambda part: part[k], everything))

    return lax.fori_loop(1, lax.axis_size(axis), hop, leading)


def combine_stats(first, second):
    top_value = jnp.maximum(first[0], second[0])
    first_factor = jnp.exp(first[0] - top_value)
    second_factor = jnp.exp(second[0] - top_value)
    return (
        top_value,
        first[1] * first_factor + second[1] * second_factor,
        first[2] * first_factor + second[2] * second_factor,
    )


def local_grads(query_rows, grad_rows, key_rows, value_rows, head_blocks, shard_index):
    row_count = query_rows.shape[0]
    query_blocks = row_count // BLOCK
    local_heads = query_rows.shape[1] // HEAD_DIM
    memory_blocks = key_rows.shape[0] // BLOCK
    slot_count = head_blocks.shape[2]
    group_size = math.gcd(query_blocks, 8)
    group_count = query_blocks // group_size
    scale = 1.0 / math.sqrt(HEAD_DIM)

    def split_queries(array):
        return array.reshape(group_count, group_size, BLOCK, local_heads, HEAD_DIM).transpose(
            3, 0, 1, 2, 4
        )

    def split_memory(array):
        return array.reshape(memory_blocks, BLOCK, local_heads, HEAD_DIM).transpose(2, 0, 1, 3)

    query_split = split_queries(query_rows)
    grad_split = split_queries(grad_rows)
    key_split = split_memory(key_rows)
    value_split = split_memory(value_rows)
    local_ids = head_blocks - shard_index * memory_blocks
    live_slots = ((local_ids >= 0) & (local_ids < memory_blocks)).reshape(
        local_heads, group_count, group_size, slot_count
    )
    slot_picks = jnp.clip(local_ids, 0, memory_blocks - 1).reshape(
        local_heads, group_count, group_size, slot_count
    )

    def block_scores(query_group, grad_group, key_head, value_head, picks):
        key_blocks = key_head[picks]
        value_blocks = value_head[picks]
        scores = (
            jnp.einsum(
                "gbd,gskd->gbsk", query_group, key_blocks, preferred_element_type=jnp.float32
            )
            * scale
        )
        prod_grad = jnp.einsum(
            "gbd,gskd->gbsk", grad_group, value_blocks, preferred_element_type=jnp.float32
        )
        return (scores, prod_grad, key_blocks)

    def stats_head(head_inputs):
        query_head, grad_head, key_head, value_head, pick_head, live_head = head_inputs

        def stats_group(group_inputs):
            query_group, grad_group, picks, live_group = group_inputs
            scores, prod_grad, unused_keys = block_scores(
                query_group, grad_group, key_head, value_head, picks
            )
            live_mask = live_group[:, None, :, None]
            top_value = jnp.max(jnp.where(live_mask, scores, -1e30), axis=(2, 3))
            weight = jnp.where(live_mask, jnp.exp(scores - top_value[:, :, None, None]), 0.0)
            return (
                top_value,
                jnp.sum(weight, axis=(2, 3)),
                jnp.sum(weight * prod_grad, axis=(2, 3)),
            )

        return lax.map(stats_group, (query_head, grad_head, pick_head, live_head))

    top_value, total, weighted = lax.map(
        stats_head, (query_split, grad_split, key_split, value_split, slot_picks, live_slots)
    )
    top_value, total, weighted = joined((top_value, total, weighted), "memory", combine_stats)
    log_total = top_value + jnp.log(total)
    delta_row = weighted / total

    def grads_head(head_inputs):
        query_head, grad_head, key_head, value_head, pick_head, live_head, log_head, delta_head = (
            head_inputs
        )

        def grads_group(carry, group_inputs):
            query_group, grad_group, picks, live_group, log_group, delta_group = group_inputs
            scores, prod_grad, key_blocks = block_scores(
                query_group, grad_group, key_head, value_head, picks
            )
            live_mask = live_group[:, None, :, None]
            probs = jnp.where(live_mask, jnp.exp(scores - log_group[:, :, None, None]), 0.0)
            probs_half = probs.astype(jnp.bfloat16)
            score_grad = (probs * (prod_grad - delta_group[:, :, None, None])).astype(jnp.bfloat16)
            value_terms = jnp.einsum(
                "gbsk,gbd->gskd", probs_half, grad_group, preferred_element_type=jnp.float32
            )
            key_terms = (
                jnp.einsum(
                    "gbsk,gbd->gskd", score_grad, query_group, preferred_element_type=jnp.float32
                )
                * scale
            )
            query_terms = (
                jnp.einsum(
                    "gbsk,gskd->gbd", score_grad, key_blocks, preferred_element_type=jnp.float32
                )
                * scale
            )
            flat_picks = picks.reshape(-1)
            flat_live = live_group.reshape(-1)[:, None, None]
            key_total = (
                carry[0]
                .at[flat_picks]
                .add(jnp.where(flat_live, key_terms.reshape(-1, BLOCK, HEAD_DIM), 0.0))
            )
            value_total = (
                carry[1]
                .at[flat_picks]
                .add(jnp.where(flat_live, value_terms.reshape(-1, BLOCK, HEAD_DIM), 0.0))
            )
            return ((key_total, value_total), query_terms)

        zero_grad = jnp.zeros((memory_blocks, BLOCK, HEAD_DIM), jnp.float32)
        totals, query_terms = lax.scan(
            grads_group,
            (zero_grad, zero_grad),
            (query_head, grad_head, pick_head, live_head, log_head, delta_head),
        )
        return (query_terms, totals[0], totals[1])

    query_grad, key_grad, value_grad = lax.map(
        grads_head,
        (
            query_split,
            grad_split,
            key_split,
            value_split,
            slot_picks,
            live_slots,
            log_total,
            delta_row,
        ),
    )
    query_grad = query_grad.transpose(1, 2, 3, 0, 4).reshape(row_count, local_heads * HEAD_DIM)
    key_grad = key_grad.transpose(1, 2, 0, 3).reshape(memory_blocks * BLOCK, local_heads * HEAD_DIM)
    value_grad = value_grad.transpose(1, 2, 0, 3).reshape(
        memory_blocks * BLOCK, local_heads * HEAD_DIM
    )
    return (query_grad, key_grad, value_grad)


def shards(queries, keys, values, grad_out, blocks):
    query_span, grad_span = (
        lax.all_gather(queries, "memory", axis=0, tiled=True),
        lax.all_gather(grad_out, "memory", axis=0, tiled=True),
    )
    query_index = lax.axis_index("query")
    memory_index = lax.axis_index("memory")
    key_rows, value_rows = (
        lax.all_gather(keys, "query", axis=1, tiled=True),
        lax.all_gather(values, "query", axis=1, tiled=True),
    )
    span_blocks = query_span.shape[0] // BLOCK
    head_blocks = lax.dynamic_slice_in_dim(blocks, query_index * span_blocks, span_blocks, 1)
    query_part, key_full, value_full = local_grads(
        query_span, grad_span, key_rows, value_rows, head_blocks, memory_index
    )
    key_grad, value_grad = (
        lax.psum_scatter(key_full, "query", scatter_dimension=1, tiled=True),
        lax.psum_scatter(value_full, "query", scatter_dimension=1, tiled=True),
    )
    grad_query = lax.psum_scatter(
        query_part.astype(jnp.bfloat16), "memory", scatter_dimension=0, tiled=True
    )
    return (grad_query, key_grad.astype(jnp.bfloat16), value_grad.astype(jnp.bfloat16))


def solution(mesh):
    placed = (
        P(("group", "query", "memory"), None),
        P(("group", "memory"), "query"),
        P(("group", "memory"), "query"),
        P(("group", "query", "memory"), None),
        P(None, "group", None),
    )
    return jax.shard_map(
        shards,
        mesh=mesh,
        in_specs=placed,
        out_specs=(
            P(("group", "query", "memory"), None),
            P(("group", "memory"), "query"),
            P(("group", "memory"), "query"),
        ),
        check_vma=False,
    )
```

profile of v0, /device:TPU:0, one launch (start us, length us, event | category | flops | bytes accessed | tf_op | source)
XLA Modules:
  0.0 721.9 jit_solution(12204486029570501064)
XLA Ops:
  10.6 47.6 %all-gather.8.cloned.1.call-done = bf16[512,2048]{1,0:T(8,128)(2,1)} async-done(((bf16[128,2048]{1,0:T(8,128)(2,1)}), bf16[512,2048]{1,0:T(8,128)(2,1)}) %all-gather.8.cloned.1.call-update) | async-done | bytes 2097168 | tf_op jit(solution)/shard_map/all_gather | solution.py:177
  58.3 2.2 copy.101
  60.5 1.9 copy.85
  62.4 42.1 %all-gather.12.cloned.1.call-done = bf16[512,2048]{1,0:T(8,128)(2,1)} async-done(((bf16[128,2048]{1,0:T(8,128)(2,1)}), bf16[512,2048]{1,0:T(8,128)(2,1)}) %all-gather.12.cloned.1.call-update) | async-done | bytes 2097168 | tf_op jit(solution)/shard_map/all_gather | solution.py:178
  104.5 2.2 copy.103
  106.7 1.9 copy.79
  108.6 30.7 %all-gather.10.cloned.1.call-done = bf16[1024,2048]{1,0:T(8,128)(2,1)} async-done(((bf16[1024,512]{1,0:T(8,128)(2,1)}), bf16[1024,2048]{1,0:T(8,128)(2,1)}) %all-gather.10.cloned.1.call-update) | async-done | bytes 4194320 | tf_op jit(solution)/shard_map/all_gather | solution.py:183
  139.3 3.6 copy.102
  143.6 3.1 copy.86
  146.7 28.6 %all-gather.14.cloned.1.call-done = bf16[1024,2048]{1,0:T(8,128)(2,1)} async-done(((bf16[1024,512]{1,0:T(8,128)(2,1)}), bf16[1024,2048]{1,0:T(8,128)(2,1)}) %all-gather.14.cloned.1.call-update) | async-done | bytes 4194320 | tf_op jit(solution)/shard_map/all_gather | solution.py:184
  175.2 3.6 copy.104
  179.6 3.1 copy.80
  182.6 80.8 %while.40 = (s32[]{:T(128)}, f32[16,1,4,128]{3,2,1,0:T(4,128)S(1)}, f32[16,1,4,128]{3,2,1,0:T(4,128)S(1)}, f32[16,1,4,128]{3,2,1,0:T(4,128)S(1)}, pred[16,1,4,2]...) while((s32[]{:T(128)}, f32[16,1,4,128]{3,2,1,0:T(4,128)S(1)}, ...), condition=%wide.region_4.5_spmd, body=%wide.region_0.4_spmd.sunk | while | flops 68419096 | bytes 4483549 | solution.py:96
  263.4 13.4 %all-gather.2 = f32[64,1,4,128]{3,2,1,0:T(4,128)S(1)} all-gather(f32[16,1,4,128]{3,2,1,0:T(4,128)S(1)} %get-tuple-element.367), channel_id=4, replica_groups=mesh['group'=2,'query'=4,'memory'=4] {'memory'}, dimensions={0}, use_global_device_ids=true | all-gather | bytes 163840 | tf_op jit(solution)/shard_map/all_gather | solution.py:13
  276.9 13.6 %all-gather = f32[64,1,4,128]{3,2,1,0:T(4,128)S(1)} all-gather(f32[16,1,4,128]{3,2,1,0:T(4,128)S(1)} %get-tuple-element.365), channel_id=2, replica_groups=mesh['group'=2,'query'=4,'memory'=4] {'memory'}, dimensions={0}, use_global_device_ids=true | all-gather | bytes 163840 | tf_op jit(solution)/shard_map/all_gather | solution.py:13
  290.5 13.6 %all-gather.1 = f32[64,1,4,128]{3,2,1,0:T(4,128)S(1)} all-gather(f32[16,1,4,128]{3,2,1,0:T(4,128)S(1)} %get-tuple-element.366), channel_id=3, replica_groups=mesh['group'=2,'query'=4,'memory'=4] {'memory'}, dimensions={0}, use_global_device_ids=true | all-gather | bytes 163840 | tf_op jit(solution)/shard_map/all_gather | solution.py:13
  304.6 201.8 %while.42 = (s32[]{:T(128)}, bf16[16,1,4,128,128]{4,3,2,1,0:T(8,128)(2,1)}, f32[16,8,128,128]{3,2,1,0:T(8,128)}, f32[16,8,128,128]{3,2,1,0:T(8,128)}, pred[16,1,...) while((s32[]{:T(128)}, ...), condition=%wide.region_10.11_spmd, body=%wide.region_7.10_spmd.sunk | while | flops 169411632 | bytes 15483753 | solution.py:154
  310.6 1.2 fusion.98
  311.8 1.2 convolution_multiply_fusion.5
  323.2 1.2 fusion.98
  324.4 1.2 convolution_multiply_fusion.5
  335.8 1.2 fusion.98
  337.0 1.2 convolution_multiply_fusion.5
  348.4 1.2 fusion.98
  349.6 1.2 convolution_multiply_fusion.5
  358.7 1.2 fusion.93
  361.0 1.2 fusion.98
  362.2 1.2 convolution_multiply_fusion.5
  373.7 1.2 fusion.98
  374.8 1.2 convolution_multiply_fusion.5
  386.3 1.2 fusion.98
  387.4 1.2 convolution_multiply_fusion.5
  396.5 1.2 fusion.93
  398.8 1.2 fusion.98
  400.0 1.2 convolution_multiply_fusion.5
  411.4 1.2 fusion.98
  412.6 1.2 convolution_multiply_fusion.5
  424.1 1.2 fusion.98
  425.3 1.2 convolution_multiply_fusion.5
  436.7 1.2 fusion.98
  437.9 1.2 convolution_multiply_fusion.5
  449.3 1.2 fusion.98
  450.5 1.2 convolution_multiply_fusion.5
  461.9 1.2 fusion.98
  463.1 1.2 convolution_multiply_fusion.5
  472.2 1.2 fusion.93
  474.5 1.2 fusion.98
  475.7 1.2 convolution_multiply_fusion.5
  487.1 1.2 fusion.98
  488.3 1.2 convolution_multiply_fusion.5
  499.7 1.2 fusion.98
  500.9 1.2 convolution_multiply_fusion.5
  506.3 8.1 %copy.92 = f32[8,128,16,128]{3,2,1,0:T(8,128)S(1)} copy(f32[8,128,16,128]{3,1,0,2:T(8,128)} %bitcast.259) | data formatting | bytes 16777216 | tf_op jit(solution)/shard_map/transpose | solution.py:169
  514.4 7.3 %copy.111 = f32[128,8,16,128]{3,1,2,0:T(8,128)} copy(f32[128,8,16,128]{3,2,1,0:T(8,128)S(1)} %bitcast.253) | data formatting | bytes 16777216
  522.1 8.1 %copy.91 = f32[8,128,16,128]{3,2,1,0:T(8,128)S(1)} copy(f32[8,128,16,128]{3,1,0,2:T(8,128)} %bitcast.260) | data formatting | bytes 16777216 | tf_op jit(solution)/shard_map/transpose | solution.py:168
  530.2 8.0 %copy.112 = f32[128,8,16,128]{3,1,2,0:T(8,128)} copy(f32[128,8,16,128]{3,2,1,0:T(8,128)S(1)} %bitcast.254) | data formatting | bytes 16777216
  538.3 1.5 copy-done.2
  539.8 1.4 copy.90
  541.2 1.9 copy.113
  543.0 50.9 %reduce-scatter.8.cloned.1.call-done = f32[1024,512]{1,0:T(8,128)} async-done(((f32[1024,2048]{1,0:T(8,128)}), f32[1024,512]{1,0:T(8,128)}) %reduce-scatter.8.cloned.1.call-update) | async-done | bytes 2097168 | tf_op jit(solution)/shard_map/reduce_scatter | solution.py:193
  593.9 2.7 convert_element_type.27
  596.6 71.7 %reduce-scatter.6.cloned.1.call-done = f32[1024,512]{1,0:T(8,128)} async-done(((f32[1024,2048]{1,0:T(8,128)}), f32[1024,512]{1,0:T(8,128)}) %reduce-scatter.6.cloned.1.call-update) | async-done | bytes 2097168 | tf_op jit(solution)/shard_map/reduce_scatter | solution.py:192
  668.3 2.7 convert_element_type.26
  671.0 44.1 %reduce-scatter.4.cloned.1.call-done = bf16[128,2048]{1,0:T(8,128)(2,1)} async-done(((bf16[512,2048]{1,0:T(8,128)(2,1)}), bf16[128,2048]{1,0:T(8,128)(2,1)}) %reduce-scatter.4.cloned.1.call-update) | async-done | bytes 524304 | tf_op jit(solution)/shard_map/reduce_scatter | solution.py:195
  (685 shorter events, 244.2 us)
Async XLA Ops:
  7.2 2.9 copy-start
  7.2 51.1 %all-gather.8.cloned.1.call-start = ((), (), s32[]{:S(2)}) async-start(), calls=%async_computation.3 | async-start | bytes 2621440 | tf_op jit(solution)/shard_map/all_gather | solution.py:177
  7.9 96.6 %all-gather.12.cloned.1.call-start = ((), (), s32[]{:S(2)}) async-start(), calls=%async_computation.5 | async-start | bytes 2621440 | tf_op jit(solution)/shard_map/all_gather | solution.py:178
  8.7 130.6 %all-gather.10.cloned.1.call-start = ((), (), s32[]{:S(2)}) async-start(), calls=%async_computation.4 | async-start | bytes 5242880 | tf_op jit(solution)/shard_map/all_gather | solution.py:183
  9.4 165.8 %all-gather.14.cloned.1.call-start = ((), (), s32[]{:S(2)}) async-start(), calls=%async_computation.6 | async-start | bytes 5242880 | tf_op jit(solution)/shard_map/all_gather | solution.py:184
  10.0 584.0 %reduce-scatter.8.cloned.1.call-start = ((), (), s32[]{:S(2)}) async-start(), calls=%async_computation.9 | async-start | bytes 10485760 | tf_op jit(solution)/shard_map/reduce_scatter | solution.py:193
  521.8 146.5 %reduce-scatter.6.cloned.1.call-start = ((), (), s32[]{:S(2)}) async-start(), calls=%async_computation.8 | async-start | bytes 10485760 | tf_op jit(solution)/shard_map/reduce_scatter | solution.py:192
  538.2 1.6 copy-start.2
  538.2 176.8 %reduce-scatter.4.cloned.1.call-start = ((), (), s32[]{:S(2)}) async-start(), calls=%async_computation.7 | async-start | bytes 2621440 | tf_op jit(solution)/shard_map/reduce_scatter | solution.py:195
  543.0 172.1 %copy-start.1 = (s32[16,16,2]{1,2,0:T(2,128)S(1)}, s32[16,16,2]{1,2,0:T(2,128)}, u32[]{:S(2)}) copy-start(s32[16,16,2]{1,2,0:T(2,128)} %param.15) | copy-start | bytes 6148
Sparse Core Ops, SparseCore 0:
  9.6 48.6 all-gather.7
  59.8 44.6 all-gather.11
  106.1 33.1 all-gather.9
  140.7 34.4 all-gather.13
  521.9 71.9 reduce-scatter.7
  596.5 71.6 reduce-scatter.5
  671.2 43.8 reduce-scatter.3
where the time goes:
time: 725 us; the launch traced here: 722 us
  waiting for transfers between devices  318 us (44%)
  local copies, waits for them, and re-layouts  175 us (24%)
  matrix products  126 us (17%)
  other arithmetic  44.4 us (6%)
  blocking collectives  40.7 us (6%)
  between operations  14.3 us (2%)
    reduce_scatter x1, waiting for transfers between devices, shards(): lax.psum_scatter(key_full, 'query', scatter_dimension=1, tiled=True)  71.7 us
    reduce_scatter x1, waiting for transfers between devices, shards(): lax.psum_scatter(value_full, 'query', scatter_dimension=1, tiled=True)  50.9 us
    squeeze x48, local copies, waits for them, and re-layouts, local_grads(): lax.map(stats_head, (query_split, grad_split, key_split, value_split, slo...  48.2 us
    all_gather x1, waiting for transfers between devices, shards(): lax.all_gather(queries, 'memory', axis=0, tiled=True)  47.6 us
    reduce_scatter x1, waiting for transfers between devices, shards(): lax.psum_scatter(query_part.astype(jnp.bfloat16), 'memory', scatter_dimen...  44.1 us
    all_gather x1, waiting for transfers between devices, shards(): lax.all_gather(grad_out, 'memory', axis=0, tiled=True)  42.1 us
    all_gather x3, blocking collectives, joined(): everything = jax.tree.map(lambda part: lax.all_gather(part, axis), value)  40.7 us
    dot_general x32, matrix products, block_scores(): jnp.einsum('gbd,gskd->gbsk', query_group, key_blocks, preferred_element_t...  37.2 us
  transfers between devices with their start and end apart: 7, of which 7 were waited for; matrix products, arithmetic and copies ran while one was open for 6% of the time, Pallas kernels for 0%

commit v1 on v0

--- a/solution.py
+++ b/solution.py
@@ -1,8 +1,11 @@
+import functools
 import math
 
 import jax
 import jax.numpy as jnp
 from jax import lax
+from jax.experimental import pallas as pl
+from jax.experimental.pallas import tpu as pltpu
 from jax.sharding import PartitionSpec as P
 
 HEAD_DIM = 128
@@ -172,7 +175,7 @@
     return (query_grad, key_grad, value_grad)
 
 
-def shards(queries, keys, values, grad_out, blocks):
+def span_shards(queries, keys, values, grad_out, blocks):
     query_span, grad_span = (
         lax.all_gather(queries, "memory", axis=0, tiled=True),
         lax.all_gather(grad_out, "memory", axis=0, tiled=True),
@@ -196,6 +199,259 @@
         query_part.astype(jnp.bfloat16), "memory", scatter_dimension=0, tiled=True
     )
     return (grad_query, key_grad.astype(jnp.bfloat16), value_grad.astype(jnp.bfloat16))
+
+
+MESH = pl.DeviceIdType.MESH
+NT = (((1,), (1,)), ((), ()))
+TN = (((0,), (0,)), ((), ()))
+
+
+def position():
+    memory_size = lax.axis_size("memory")
+    here = lax.axis_index("query") * memory_size + lax.axis_index("memory")
+    return lax.axis_index("group"), here, memory_size
+
+
+def meet(group, here, devices, memory_size):
+    barrier = pltpu.get_barrier_semaphore()
+    for step in range(1, devices):
+        peer = lax.rem(here + step, devices)
+        pl.semaphore_signal(
+            barrier,
+            inc=1,
+            device_id=(group, peer // memory_size, lax.rem(peer, memory_size)),
+            device_id_type=MESH,
+        )
+    pl.semaphore_wait(barrier, devices - 1)
+
+
+def columns(index):
+    return pl.ds(pl.multiple_of(index * HEAD_DIM, HEAD_DIM), HEAD_DIM)
+
+
+def rows(index, size):
+    return pl.ds(pl.multiple_of(index * size, size), size)
+
+
+def to_heads_kernel(
+    devices, query_ref, grad_ref, key_ref, value_ref, query_out, grad_out, key_out, value_out,
+    send_sem, recv_sem, own_sem,
+):
+    group, here, memory_size = position()
+    my_query, my_memory = here // memory_size, lax.rem(here, memory_size)
+    row_count, memory_rows = query_ref.shape[0], key_ref.shape[0]
+    meet(group, here, devices, memory_size)
+    copies = []
+    for step in range(1, memory_size):
+        peer = lax.rem(my_memory + step, memory_size)
+        for which, (source, target) in enumerate(((key_ref, key_out), (value_ref, value_out))):
+            slot = 2 * devices + which * memory_size + step
+            copy = pltpu.make_async_remote_copy(
+                src_ref=source.at[:, columns(peer)],
+                dst_ref=target.at[rows(my_memory, memory_rows), :],
+                send_sem=send_sem.at[slot],
+                recv_sem=recv_sem.at[slot],
+                device_id=(group, my_query, peer),
+                device_id_type=MESH,
+            )
+            copy.start()
+            copies.append(copy)
+    for step in range(1, devices):
+        peer = lax.rem(here + step, devices)
+        for which, (source, target) in enumerate(((query_ref, query_out), (grad_ref, grad_out))):
+            slot = which * devices + step
+            copy = pltpu.make_async_remote_copy(
+                src_ref=source.at[:, columns(peer)],
+                dst_ref=target.at[rows(here, row_count), :],
+                send_sem=send_sem.at[slot],
+                recv_sem=recv_sem.at[slot],
+                device_id=(group, peer // memory_size, lax.rem(peer, memory_size)),
+                device_id_type=MESH,
+            )
+            copy.start()
+            copies.append(copy)
+    own = [
+        pltpu.make_async_copy(
+            query_ref.at[:, columns(here)], query_out.at[rows(here, row_count), :], own_sem.at[0]
+        ),
+        pltpu.make_async_copy(
+            grad_ref.at[:, columns(here)], grad_out.at[rows(here, row_count), :], own_sem.at[1]
+        ),
+        pltpu.make_async_copy(
+            key_ref.at[:, columns(my_memory)], key_out.at[rows(my_memory, memory_rows), :], own_sem.at[2]
+        ),
+        pltpu.make_async_copy(
+            value_ref.at[:, columns(my_memory)], value_out.at[rows(my_memory, memory_rows), :], own_sem.at[3]
+        ),
+    ]
+    for copy in own:
+        copy.start()
+    for copy in own:
+        copy.wait()
+    for copy in copies:
+        copy.wait()
+
+
+def from_heads_kernel(
+    devices, query_ref, key_ref, value_ref, query_out, key_out, value_out,
+    send_sem, recv_sem, own_sem,
+):
+    group, here, memory_size = position()
+    my_query, my_memory = here // memory_size, lax.rem(here, memory_size)
+    row_count, memory_rows = query_out.shape[0], key_out.shape[0]
+    meet(group, here, devices, memory_size)
+    copies = []
+    for step in range(1, memory_size):
+        peer = lax.rem(my_memory + step, memory_size)
+        for which, (source, target) in enumerate(((key_ref, key_out), (value_ref, value_out))):
+            slot = devices + which * memory_size + step
+            copy = pltpu.make_async_remote_copy(
+                src_ref=source.at[rows(peer, memory_rows), :],
+                dst_ref=target.at[:, columns(my_memory)],
+                send_sem=send_sem.at[slot],
+                recv_sem=recv_sem.at[slot],
+                device_id=(group, my_query, peer),
+                device_id_type=MESH,
+            )
+            copy.start()
+            copies.append(copy)
+    for step in range(1, devices):
+        peer = lax.rem(here + step, devices)
+        copy = pltpu.make_async_remote_copy(
+            src_ref=query_ref.at[rows(peer, row_count), :],
+            dst_ref=query_out.at[:, columns(here)],
+            send_sem=send_sem.at[step],
+            recv_sem=recv_sem.at[step],
+            device_id=(group, peer // memory_size, lax.rem(peer, memory_size)),
+            device_id_type=MESH,
+        )
+        copy.start()
+        copies.append(copy)
+    own = [
+        pltpu.make_async_copy(
+            query_ref.at[rows(here, row_count), :], query_out.at[:, columns(here)], own_sem.at[0]
+        ),
+        pltpu.make_async_copy(
+            key_ref.at[rows(my_memory, memory_rows), :], key_out.at[:, columns(my_memory)], own_sem.at[1]
+        ),
+        pltpu.make_async_copy(
+            value_ref.at[rows(my_memory, memory_rows), :], value_out.at[:, columns(my_memory)], own_sem.at[2]
+        ),
+    ]
+    for copy in own:
+        copy.start()
+    for copy in own:
+        copy.wait()
+    for copy in copies:
+        copy.wait()
+
+
+def head_kernel(
+    picks, query_ref, grad_ref, key_ref, value_ref, query_out, key_out, value_out,
+    key_total, value_total,
+):
+    scale = 1.0 / math.sqrt(HEAD_DIM)
+    key_total[...] = jnp.zeros_like(key_total)
+    value_total[...] = jnp.zeros_like(value_total)
+
+    def block(index, carry):
+        here = rows(index, BLOCK)
+        places = [rows(picks[index, slot], BLOCK) for slot in range(2)]
+        query, grad = query_ref[here, :], grad_ref[here, :]
+        keys = jnp.concatenate([key_ref[place, :] for place in places], axis=0)
+        values = jnp.concatenate([value_ref[place, :] for place in places], axis=0)
+        scores = lax.dot_general(query, keys, NT, preferred_element_type=jnp.float32) * scale
+        prod_grad = lax.dot_general(grad, values, NT, preferred_element_type=jnp.float32)
+        weight = jnp.exp(scores - jnp.max(scores, axis=1, keepdims=True))
+        probs = weight / jnp.sum(weight, axis=1, keepdims=True)
+        delta = jnp.sum(probs * prod_grad, axis=1, keepdims=True)
+        probs_half = probs.astype(jnp.bfloat16)
+        score_grad = (probs * (prod_grad - delta)).astype(jnp.bfloat16)
+        query_out[here, :] = (
+            lax.dot_general(
+                score_grad, keys, (((1,), (0,)), ((), ())), preferred_element_type=jnp.float32
+            )
+            * scale
+        ).astype(query_out.dtype)
+        value_terms = lax.dot_general(probs_half, grad, TN, preferred_element_type=jnp.float32)
+        key_terms = lax.dot_general(score_grad, query, TN, preferred_element_type=jnp.float32)
+        for slot, place in enumerate(places):
+            part = slice(slot * BLOCK, (slot + 1) * BLOCK)
+            key_total[place, :] += key_terms[part]
+            value_total[place, :] += value_terms[part]
+        return carry
+
+    lax.fori_loop(0, query_ref.shape[0] // BLOCK, block, 0, unroll=2)
+    key_out[...] = (key_total[...] * scale).astype(key_out.dtype)
+    value_out[...] = value_total[...].astype(value_out.dtype)
+
+
+def head_shards(queries, keys, values, grad_out, blocks):
+    memory_size = lax.axis_size("memory")
+    devices = lax.axis_size("query") * memory_size
+    row_count, memory_rows = queries.shape[0], keys.shape[0]
+    all_rows, all_memory = row_count * devices, memory_rows * memory_size
+    anywhere, vmem = pl.BlockSpec(memory_space=pl.ANY), pl.BlockSpec(memory_space=pltpu.VMEM)
+
+    def like(*shape):
+        return jax.ShapeDtypeStruct(shape, jnp.bfloat16)
+
+    def semaphores(count, own):
+        return [
+            pltpu.SemaphoreType.DMA((count,)),
+            pltpu.SemaphoreType.DMA((count,)),
+            pltpu.SemaphoreType.DMA((own,)),
+        ]
+
+    query_head, grad_head, key_head, value_head = pl.pallas_call(
+        functools.partial(to_heads_kernel, devices),
+        out_shape=(
+            like(all_rows, HEAD_DIM),
+            like(all_rows, HEAD_DIM),
+            like(all_memory, HEAD_DIM),
+            like(all_memory, HEAD_DIM),
+        ),
+        in_specs=[anywhere] * 4,
+        out_specs=(anywhere,) * 4,
+        scratch_shapes=semaphores(2 * devices + 2 * memory_size, 4),
+        compiler_params=pltpu.CompilerParams(collective_id=0, has_side_effects=True),
+        name="to_heads",
+    )(queries, grad_out, keys, values)
+    head = lax.axis_index("query") * memory_size + lax.axis_index("memory")
+    picks = lax.dynamic_index_in_dim(blocks, head, 0, keepdims=False)
+    query_grad, key_grad, value_grad = pl.pallas_call(
+        head_kernel,
+        out_shape=(
+            like(all_rows, HEAD_DIM),
+            like(all_memory, HEAD_DIM),
+            like(all_memory, HEAD_DIM),
+        ),
+        in_specs=[pl.BlockSpec(memory_space=pltpu.SMEM)] + [vmem] * 4,
+        out_specs=(vmem,) * 3,
+        scratch_shapes=[pltpu.VMEM((all_memory, HEAD_DIM), jnp.float32)] * 2,
+        compiler_params=pltpu.CompilerParams(vmem_limit_bytes=32 * 1024 * 1024),
+        name="head_grads",
+    )(picks, query_head, grad_head, key_head, value_head)
+    return pl.pallas_call(
+        functools.partial(from_heads_kernel, devices),
+        out_shape=(
+            like(row_count, queries.shape[1]),
+            like(memory_rows, keys.shape[1]),
+            like(memory_rows, keys.shape[1]),
+        ),
+        in_specs=[anywhere] * 3,
+        out_specs=(anywhere,) * 3,
+        scratch_shapes=semaphores(devices + 2 * memory_size, 3),
+        compiler_params=pltpu.CompilerParams(collective_id=1, has_side_effects=True),
+        name="from_heads",
+    )(query_grad, key_grad, value_grad)
+
+
+def shards(queries, keys, values, grad_out, blocks):
+    devices = lax.axis_size("query") * lax.axis_size("memory")
+    if devices == blocks.shape[0]:
+        return head_shards(queries, keys, values, grad_out, blocks)
+    return span_shards(queries, keys, values, grad_out, blocks)
 
 
 def solution(mesh):

time: 725 us -> 160 us (0.22)
  waiting for transfers between devices: 318 us -> 0 us
  local copies, waits for them, and re-layouts: 175 us -> 12.6 us
  Pallas kernels: 0 us -> 146 us
  matrix products: 126 us -> 0 us
  other arithmetic: 44.4 us -> 0 us
  blocking collectives: 40.7 us -> 0 us
  between operations: 14.3 us -> 0.7 us
    reduce_scatter x3 -> x0, waiting for transfers between devices: 167 us -> none  [the longest x1 71.7 us: shards(): lax.psum_scatter(key_full, 'query', scatter_dimension=1, tiled=True)]
    all_gather x4 -> x0, waiting for transfers between devices: 149 us -> none  [the longest x1 47.6 us: shards(): lax.all_gather(queries, 'memory', axis=0, tiled=True)]
    pallas_call x0 -> x3, Pallas kernels: none -> 146 us  [the longest x1 74.9 us: head_shards(): pl.pallas_call(functools.partial(to_heads_kernel, devices), out_shape=(li...]
    dot_general x112 -> x0, matrix products: 126 us -> none  [the longest x32 37.2 us: block_scores(): jnp.einsum('gbd,gskd->gbsk', query_group, key_blocks, preferred_element_t...]
    squeeze x48 -> x2, local copies, waits for them, and re-layouts: 48.2 us -> 0.09 us  [head_shards(): picks = lax.dynamic_index_in_dim(blocks, head, 0, keepdims=False)]
    all_gather x3 -> x0, blocking collectives: 40.7 us -> none  [joined(): everything = jax.tree.map(lambda part: lax.all_gather(part, axis), value)]
    gather x64 -> x0, local copies, waits for them, and re-layouts: 38.2 us -> none  [the longest x32 19.1 us: block_scores(): key_blocks = key_head[picks]]
    scatter-add x32 -> x0, other arithmetic: 32.9 us -> none  [the longest x16 16.5 us: grads_group(): key_total = carry[0].at[flat_picks].add(jnp.where(flat_live, key_terms.re...]
  transfers between devices with their start and end apart: 7 -> 0, of which waited for: 7 -> 0; matrix products, arithmetic and copies ran while one was open for 6% -> 0% of each run, Pallas kernels for 0% -> 0%
where the time goes in v1:
time: 160 us; the launch traced here: 159 us
  Pallas kernels  146 us (91%)
  local copies, waits for them, and re-layouts  12.6 us (8%)
    pallas_call x1, Pallas kernels, head_shards(): pl.pallas_call(functools.partial(to_heads_kernel, devices), out_shape=(li...  74.9 us
    pallas_call x1, Pallas kernels, head_shards(): pl.pallas_call(functools.partial(from_heads_kernel, devices), out_shape=(...  61.8 us
    unnamed x23, local copies, waits for them, and re-layouts  12.5 us
    pallas_call x1, Pallas kernels, head_shards(): pl.pallas_call(head_kernel, out_shape=(like(all_rows, HEAD_DIM), like(all...  9.39 us

profile of v1, /device:TPU:0, one launch (start us, length us, event | category | flops | bytes accessed | tf_op | source)
XLA Modules:
  0.0 159.4 jit_solution(17925547195729532752)
XLA Ops:
  0.6 0.0 copy-start
  0.7 0.7 copy-done
  1.4 0.1 copy.8.picks
  1.4 74.9 %to_heads.1 = (bf16[2048,128]{1,0:T(8,128)(2,1)}, bf16[2048,128]{1,0:T(8,128)(2,1)}, bf16[4096,128]{1,0:T(8,128)(2,1)}, bf16[4096,128]{1,0:T(8,128)(2,1)}) custom-call(bf16[128,2048]{1,0:T(8,128)(2,1)} %query_ref.1, bf16[128,2048]{1,0:T(8,128)(2,1)} %grad_ref.1, bf16[1024,512]{1,0:T(8,128)(2,1)} %key_ref.1, bf16[1024,512]{1,0:T(8,128)(2,1)} %value_ref.1), custom_call_target="tpu_custom_call" | custom-call | tf_op jit(solution)/shard_map/to_heads/pallas_call | solution.py:406
  76.4 0.0 copy-start.1
  76.4 1.2 copy-done.1
  77.6 0.0 copy-start.2
  77.6 1.2 copy-done.2
  78.8 0.0 copy-start.6
  78.8 1.0 copy-done.6
  79.9 0.0 copy-start.7
  79.9 1.0 copy-done.7
  80.9 9.4 %head_grads.1 = (bf16[2048,128]{1,0:T(8,128)(2,1)S(1)}, bf16[4096,128]{1,0:T(8,128)(2,1)S(1)}, bf16[4096,128]{1,0:T(8,128)(2,1)S(1)}) custom-call(s32[16,2]{1,0:T(8,128)S(1)} %copy.8.picks, bf16[2048,128]{1,0:T(8,128)(2,1)S(1)} %copy-done.6, bf16[2048,128]{1,0:T(8,128)(2,1)S(1)} %copy-done.7, bf16[4096,128]{1,0:T(8,128)(2,1)S(1)} %copy-done.1, ...), custom_call_target="tpu_custom_call" | custom-call | tf_op jit(solution)/shard_map/head_grads/pallas_call | solution.py:422
  90.3 0.0 copy-start.3
  90.3 1.0 copy-done.3
  91.3 0.0 copy-start.4
  91.3 1.0 copy-done.4
  92.3 0.0 copy-start.5
  92.3 0.8 copy-done.5
  93.1 61.8 %from_heads.1 = (bf16[128,2048]{1,0:T(8,128)(2,1)}, bf16[1024,512]{1,0:T(8,128)(2,1)}, bf16[1024,512]{1,0:T(8,128)(2,1)}) custom-call(bf16[2048,128]{1,0:T(8,128)(2,1)} %copy-done.5, bf16[4096,128]{1,0:T(8,128)(2,1)} %copy-done.3, bf16[4096,128]{1,0:T(8,128)(2,1)} %copy-done.4), custom_call_target="tpu_custom_call" | custom-call | tf_op jit(solution)/shard_map/from_heads/pallas_call | solution.py:435
  154.9 0.0 copy-start.9
  154.9 2.0 %copy.12 = bf16[128,2048]{1,0:T(8,128)(2,1)} copy(bf16[128,2048]{1,0:T(8,128)(2,1)} %get-tuple-element.20) | data formatting | bytes 1048576
  156.9 0.0 copy-done.9
  156.9 0.0 copy-start.8
  156.9 1.0 copy.13
  157.8 0.6 copy-done.8
  158.5 1.0 copy.14
  (1 shorter events, 0.0 us)
Async XLA Ops:
  0.6 0.7 copy-start
  76.4 1.2 copy-start.1
  77.6 1.2 copy-start.2
  78.8 1.0 copy-start.6
  79.9 1.0 copy-start.7
  90.3 1.0 copy-start.3
  91.3 1.0 copy-start.4
  92.3 0.8 copy-start.5
  154.9 2.0 %copy-start.9 = (bf16[1024,512]{1,0:T(8,128)(2,1)S(1)}, bf16[1024,512]{1,0:T(8,128)(2,1)}, u32[]{:S(2)}) copy-start(bf16[1024,512]{1,0:T(8,128)(2,1)} %get-tuple-element.21) | copy-start | bytes 3145732
  156.9 1.6 %copy-start.8 = (bf16[1024,512]{1,0:T(8,128)(2,1)S(1)}, bf16[1024,512]{1,0:T(8,128)(2,1)}, u32[]{:S(2)}) copy-start(bf16[1024,512]{1,0:T(8,128)(2,1)} %get-tuple-element.22) | copy-start | bytes 3145732

commit v2 on v0

--- a/solution.py
+++ b/solution.py
@@ -1,8 +1,11 @@
+import functools
 import math
 
 import jax
 import jax.numpy as jnp
 from jax import lax
+from jax.experimental import pallas as pl
+from jax.experimental.pallas import tpu as pltpu
 from jax.sharding import PartitionSpec as P
 
 HEAD_DIM = 128
@@ -172,7 +175,7 @@
     return (query_grad, key_grad, value_grad)
 
 
-def shards(queries, keys, values, grad_out, blocks):
+def span_shards(queries, keys, values, grad_out, blocks):
     query_span, grad_span = (
         lax.all_gather(queries, "memory", axis=0, tiled=True),
         lax.all_gather(grad_out, "memory", axis=0, tiled=True),
@@ -196,6 +199,380 @@
         query_part.astype(jnp.bfloat16), "memory", scatter_dimension=0, tiled=True
     )
     return (grad_query, key_grad.astype(jnp.bfloat16), value_grad.astype(jnp.bfloat16))
+
+
+MESH = pl.DeviceIdType.MESH
+NT = (((1,), (1,)), ((), ()))
+TN = (((0,), (0,)), ((), ()))
+UNROLL = 2
+
+
+def position():
+    memory_size = lax.axis_size("memory")
+    here = lax.axis_index("query") * memory_size + lax.axis_index("memory")
+    return lax.axis_index("group"), here, memory_size
+
+
+def meet(group, here, devices, memory_size):
+    barrier = pltpu.get_barrier_semaphore()
+    for step in range(1, devices):
+        peer = lax.rem(here + step, devices)
+        pl.semaphore_signal(
+            barrier,
+            inc=1,
+            device_id=(group, peer // memory_size, lax.rem(peer, memory_size)),
+            device_id_type=MESH,
+        )
+    pl.semaphore_wait(barrier, devices - 1)
+
+
+def columns(index, width):
+    return pl.ds(pl.multiple_of(index * width, width), width)
+
+
+def rows(index, size):
+    return pl.ds(pl.multiple_of(index * size, size), size)
+
+
+def send_all(copies, own):
+    for copy in copies + own:
+        copy.start()
+    for copy in own + copies:
+        copy.wait()
+
+
+def to_heads_kernel(
+    devices, half, query_ref, grad_ref, key_ref, value_ref, query_out, grad_out, key_out, value_out,
+    send_sem, recv_sem, own_sem,
+):
+    group, here, memory_size = position()
+    my_query, my_memory = here // memory_size, lax.rem(here, memory_size)
+    row_count, memory_rows = query_ref.shape[0], key_ref.shape[0]
+    width = query_out.shape[1]
+    base, lane = my_memory // half * half, lax.rem(my_memory, half)
+    meet(group, here, devices, memory_size)
+    copies, own = [], []
+    for which, (source, target) in enumerate(((key_ref, key_out), (value_ref, value_out))):
+        for step in range(half):
+            peer = lax.rem(lane + step, half)
+            slot = 2 * devices + which * half + step
+            ends = dict(
+                src_ref=source.at[:, columns(peer, width)],
+                dst_ref=target.at[rows(lane, memory_rows), :],
+            )
+            if step == 0:
+                own.append(pltpu.make_async_copy(*ends.values(), own_sem.at[which]))
+            else:
+                copies.append(
+                    pltpu.make_async_remote_copy(
+                        **ends,
+                        send_sem=send_sem.at[slot],
+                        recv_sem=recv_sem.at[slot],
+                        device_id=(group, my_query, base + peer),
+                        device_id_type=MESH,
+                    )
+                )
+    for step in range(devices):
+        peer = lax.rem(here + step, devices)
+        peer_query, peer_memory = peer // memory_size, lax.rem(peer, memory_size)
+        part = peer_query * half + lax.rem(peer_memory, half)
+        for which, (source, target) in enumerate(((query_ref, query_out), (grad_ref, grad_out))):
+            slot = which * devices + step
+            ends = dict(
+                src_ref=source.at[:, columns(part, width)],
+                dst_ref=target.at[rows(here, row_count), :],
+            )
+            if step == 0:
+                own.append(pltpu.make_async_copy(*ends.values(), own_sem.at[2 + which]))
+            else:
+                copies.append(
+                    pltpu.make_async_remote_copy(
+                        **ends,
+                        send_sem=send_sem.at[slot],
+                        recv_sem=recv_sem.at[slot],
+                        device_id=(group, peer_query, peer_memory),
+                        device_id_type=MESH,
+                    )
+                )
+    send_all(copies, own)
+
+
+def from_heads_kernel(
+    devices, half, query_ref, key_ref, value_ref, query_out, key_out, value_out, parts,
+    send_sem, recv_sem, own_sem,
+):
+    group, here, memory_size = position()
+    my_query, my_memory = here // memory_size, lax.rem(here, memory_size)
+    row_count, memory_rows = query_out.shape[0], key_out.shape[0]
+    width = query_ref.shape[1]
+    side, lane = my_memory // half, lax.rem(my_memory, half)
+    meet(group, here, devices, memory_size)
+    copies, own = [], []
+    for which, (source, target) in enumerate(((key_ref, key_out), (value_ref, value_out))):
+        for step in range(half):
+            peer = lax.rem(lane + step, half)
+            slot = devices + which * half + step
+            ends = dict(
+                src_ref=source.at[rows(peer, memory_rows), :],
+                dst_ref=target.at[:, columns(lane, width)],
+            )
+            if step == 0:
+                own.append(pltpu.make_async_copy(*ends.values(), own_sem.at[which]))
+            else:
+                copies.append(
+                    pltpu.make_async_remote_copy(
+                        **ends,
+                        send_sem=send_sem.at[slot],
+                        recv_sem=recv_sem.at[slot],
+                        device_id=(group, my_query, side * half + peer),
+                        device_id_type=MESH,
+                    )
+                )
+    for step in range(devices):
+        peer = lax.rem(here + step, devices)
+        ends = dict(
+            src_ref=query_ref.at[rows(peer, row_count), :],
+            dst_ref=parts.at[side, :, columns(my_query * half + lane, width)],
+        )
+        if step == 0:
+            own.append(pltpu.make_async_copy(*ends.values(), own_sem.at[2]))
+        else:
+            copies.append(
+                pltpu.make_async_remote_copy(
+                    **ends,
+                    send_sem=send_sem.at[step],
+                    recv_sem=recv_sem.at[step],
+                    device_id=(group, peer // memory_size, lax.rem(peer, memory_size)),
+                    device_id_type=MESH,
+                )
+            )
+    send_all(copies, own)
+    total = parts[0].astype(jnp.float32) + parts[1].astype(jnp.float32)
+    query_out[...] = total.astype(query_out.dtype)
+
+
+def combine_kernel(half, stats_ref, out_ref, other, send_sem, recv_sem):
+    group, here, memory_size = position()
+    my_query, my_memory = here // memory_size, lax.rem(here, memory_size)
+    partner = (group, my_query, lax.rem(my_memory + half, memory_size))
+    barrier = pltpu.get_barrier_semaphore()
+    pl.semaphore_signal(barrier, inc=1, device_id=partner, device_id_type=MESH)
+    pl.semaphore_wait(barrier, 1)
+    copy = pltpu.make_async_remote_copy(
+        src_ref=stats_ref,
+        dst_ref=other,
+        send_sem=send_sem,
+        recv_sem=recv_sem,
+        device_id=partner,
+        device_id_type=MESH,
+    )
+    copy.start()
+    copy.wait()
+    top, total, weighted = combine_stats(
+        (stats_ref[0], stats_ref[1], stats_ref[2]), (other[0], other[1], other[2])
+    )
+    out_ref[0] = top + jnp.log(total)
+    out_ref[1] = weighted / total
+
+
+def list_live(picks, live, half_blocks):
+    def add(number, count):
+        live[count] = number
+        pick = picks[number]
+        return count + jnp.where((pick >= 0) & (pick < half_blocks), 1, 0)
+
+    return lax.fori_loop(0, picks.shape[0], add, 0)
+
+
+def pair_of(number, picks, query_blocks):
+    row = number // 2
+    head, block = row // query_blocks, lax.rem(row, query_blocks)
+    return row, columns(head, HEAD_DIM), rows(block, BLOCK), rows(picks[number], BLOCK)
+
+
+def pair_scores(query, grad, key, value):
+    scale = 1.0 / math.sqrt(HEAD_DIM)
+    scores = lax.dot_general(key, query, NT, preferred_element_type=jnp.float32) * scale
+    prod_grad = lax.dot_general(value, grad, NT, preferred_element_type=jnp.float32)
+    return scores, prod_grad
+
+
+def stats_kernel(picks, query_ref, grad_ref, key_ref, value_ref, out_ref, parts, live):
+    query_blocks = query_ref.shape[0] // BLOCK
+    parts[:, 0] = jnp.full(parts[:, 0].shape, -1e30, jnp.float32)
+    parts[:, 1:] = jnp.zeros(parts[:, 1:].shape, jnp.float32)
+    count = list_live(picks, live, key_ref.shape[0] // BLOCK)
+
+    def step(index, carry):
+        for part in range(UNROLL):
+            number = live[jnp.minimum(index * UNROLL + part, count - 1)]
+            row, head, here, there = pair_of(number, picks, query_blocks)
+            scores, prod_grad = pair_scores(
+                query_ref[here, head], grad_ref[here, head], key_ref[there, head], value_ref[there, head]
+            )
+            top = jnp.max(scores, axis=0, keepdims=True)
+            weight = jnp.exp(scores - top)
+            slot, line = lax.rem(number, 2), pl.ds(row, 1)
+            parts[slot, 0, line, :] = top
+            parts[slot, 1, line, :] = jnp.sum(weight, axis=0, keepdims=True)
+            parts[slot, 2, line, :] = jnp.sum(weight * prod_grad, axis=0, keepdims=True)
+        return carry
+
+    lax.fori_loop(0, (count + UNROLL - 1) // UNROLL, step, 0)
+    both = combine_stats(
+        (parts[0, 0], parts[0, 1], parts[0, 2]), (parts[1, 0], parts[1, 1], parts[1, 2])
+    )
+    for index in range(3):
+        out_ref[index] = both[index]
+
+
+def grads_kernel(
+    picks, stats_ref, query_ref, grad_ref, key_ref, value_ref, query_out, key_out, value_out,
+    query_total, key_total, value_total, live,
+):
+    scale = 1.0 / math.sqrt(HEAD_DIM)
+    query_blocks = query_ref.shape[0] // BLOCK
+    for total in (query_total, key_total, value_total):
+        total[...] = jnp.zeros_like(total)
+    count = list_live(picks, live, key_ref.shape[0] // BLOCK)
+
+    def step(index, carry):
+        terms = []
+        for part in range(UNROLL):
+            at = index * UNROLL + part
+            number = live[jnp.minimum(at, count - 1)]
+            row, head, here, there = pair_of(number, picks, query_blocks)
+            query, grad, key = query_ref[here, head], grad_ref[here, head], key_ref[there, head]
+            scores, prod_grad = pair_scores(query, grad, key, value_ref[there, head])
+            line = pl.ds(row, 1)
+            probs = jnp.exp(scores - stats_ref[0, line, :])
+            probs = jnp.where(at < count, probs, 0.0)
+            probs_half = probs.astype(jnp.bfloat16)
+            score_grad = (probs * (prod_grad - stats_ref[1, line, :])).astype(jnp.bfloat16)
+            plain = (((1,), (0,)), ((), ()))
+            terms.append((
+                head, here, there,
+                lax.dot_general(probs_half, grad, plain, preferred_element_type=jnp.float32),
+                lax.dot_general(score_grad, query, plain, preferred_element_type=jnp.float32),
+                lax.dot_general(score_grad, key, TN, preferred_element_type=jnp.float32),
+            ))
+        for head, here, there, value_term, key_term, query_term in terms:
+            value_total[there, head] += value_term
+            key_total[there, head] += key_term
+            query_total[here, head] += query_term
+        return carry
+
+    lax.fori_loop(0, (count + UNROLL - 1) // UNROLL, step, 0)
+    query_out[...] = (query_total[...] * scale).astype(query_out.dtype)
+    key_out[...] = (key_total[...] * scale).astype(key_out.dtype)
+    value_out[...] = value_total[...].astype(value_out.dtype)
+
+
+def head_shards(queries, keys, values, grad_out, blocks):
+    memory_size = lax.axis_size("memory")
+    devices = lax.axis_size("query") * memory_size
+    half = memory_size // 2
+    row_count, memory_rows = queries.shape[0], keys.shape[0]
+    all_rows, half_rows = row_count * devices, memory_rows * half
+    width = keys.shape[1] // half
+    heads = width // HEAD_DIM
+    stat_rows, pairs = heads * all_rows // BLOCK, 2 * heads * all_rows // BLOCK
+    anywhere, vmem = pl.BlockSpec(memory_space=pl.ANY), pl.BlockSpec(memory_space=pltpu.VMEM)
+    smem = pl.BlockSpec(memory_space=pltpu.SMEM)
+    local = pltpu.CompilerParams(vmem_limit_bytes=40 * 1024 * 1024)
+
+    def like(*shape, dtype=jnp.bfloat16):
+        return jax.ShapeDtypeStruct(shape, dtype)
+
+    def semaphores(count, own):
+        return [
+            pltpu.SemaphoreType.DMA((count,)),
+            pltpu.SemaphoreType.DMA((count,)),
+            pltpu.SemaphoreType.DMA((own,)),
+        ]
+
+    def remote(number):
+        return pltpu.CompilerParams(
+            collective_id=number, has_side_effects=True, vmem_limit_bytes=40 * 1024 * 1024
+        )
+
+    arrays = pl.pallas_call(
+        functools.partial(to_heads_kernel, devices, half),
+        out_shape=(
+            like(all_rows, width), like(all_rows, width),
+            like(half_rows, width), like(half_rows, width),
+        ),
+        in_specs=[anywhere] * 4,
+        out_specs=(anywhere,) * 4,
+        scratch_shapes=semaphores(2 * devices + 2 * half, 4),
+        compiler_params=remote(0),
+        name="to_heads",
+    )(queries, grad_out, keys, values)
+    my_query, my_memory = lax.axis_index("query"), lax.axis_index("memory")
+    first_head = (my_query * half + my_memory % half) * heads
+    picks = lax.dynamic_slice_in_dim(blocks, first_head, heads, 0).reshape(pairs)
+    picks = picks - my_memory // half * (half_rows // BLOCK)
+    stats = pl.pallas_call(
+        stats_kernel,
+        out_shape=like(3, stat_rows, BLOCK, dtype=jnp.float32),
+        in_specs=[smem] + [vmem] * 4,
+        out_specs=vmem,
+        scratch_shapes=[
+            pltpu.VMEM((2, 3, stat_rows, BLOCK), jnp.float32),
+            pltpu.SMEM((pairs,), jnp.int32),
+        ],
+        compiler_params=local,
+        name="stats",
+    )(picks, *arrays)
+    stats = pl.pallas_call(
+        functools.partial(combine_kernel, half),
+        out_shape=like(2, stat_rows, BLOCK, dtype=jnp.float32),
+        in_specs=[vmem],
+        out_specs=vmem,
+        scratch_shapes=[
+            pltpu.VMEM((3, stat_rows, BLOCK), jnp.float32),
+            pltpu.SemaphoreType.DMA,
+            pltpu.SemaphoreType.DMA,
+        ],
+        compiler_params=remote(1),
+        name="combine",
+    )(stats)
+    grads = pl.pallas_call(
+        grads_kernel,
+        out_shape=(like(all_rows, width), like(half_rows, width), like(half_rows, width)),
+        in_specs=[smem] + [vmem] * 5,
+        out_specs=(vmem,) * 3,
+        scratch_shapes=[
+            pltpu.VMEM((all_rows, width), jnp.float32),
+            pltpu.VMEM((half_rows, width), jnp.float32),
+            pltpu.VMEM((half_rows, width), jnp.float32),
+            pltpu.SMEM((pairs,), jnp.int32),
+        ],
+        compiler_params=local,
+        name="head_grads",
+    )(picks, stats, *arrays)
+    return pl.pallas_call(
+        functools.partial(from_heads_kernel, devices, half),
+        out_shape=(
+            like(row_count, queries.shape[1]),
+            like(memory_rows, keys.shape[1]),
+            like(memory_rows, keys.shape[1]),
+        ),
+        in_specs=[anywhere] * 3,
+        out_specs=(vmem, anywhere, anywhere),
+        scratch_shapes=[pltpu.VMEM((2, row_count, queries.shape[1]), jnp.bfloat16)]
+        + semaphores(devices + 2 * half, 3),
+        compiler_params=remote(2),
+        name="from_heads",
+    )(*grads)
+
+
+def shards(queries, keys, values, grad_out, blocks):
+    memory_size = lax.axis_size("memory")
+    whole_heads = keys.shape[1] % (memory_size // 2 * HEAD_DIM) == 0
+    if memory_size % 2 == 0 and whole_heads and blocks.shape[2] == 2:
+        return head_shards(queries, keys, values, grad_out, blocks)
+    return span_shards(queries, keys, values, grad_out, blocks)
 
 
 def solution(mesh):

time: 725 us -> 145 us (0.20)
  waiting for transfers between devices: 318 us -> 0 us
  local copies, waits for them, and re-layouts: 175 us -> 7.46 us
  Pallas kernels: 0 us -> 136 us
  matrix products: 126 us -> 0 us
  other arithmetic: 44.4 us -> 0.69 us
  blocking collectives: 40.7 us -> 0 us
  between operations: 14.3 us -> 0.71 us
    reduce_scatter x3 -> x0, waiting for transfers between devices: 167 us -> none  [the longest x1 71.7 us: shards(): lax.psum_scatter(key_full, 'query', scatter_dimension=1, tiled=True)]
    all_gather x4 -> x0, waiting for transfers between devices: 149 us -> none  [the longest x1 47.6 us: shards(): lax.all_gather(queries, 'memory', axis=0, tiled=True)]
    pallas_call x0 -> x5, Pallas kernels: none -> 136 us  [the longest x1 64.4 us: head_shards(): pl.pallas_call(functools.partial(to_heads_kernel, devices, half), out_sha...]
    dot_general x112 -> x0, matrix products: 126 us -> none  [the longest x32 37.2 us: block_scores(): jnp.einsum('gbd,gskd->gbsk', query_group, key_blocks, preferred_element_t...]
    squeeze x48 -> x0, local copies, waits for them, and re-layouts: 48.2 us -> none  [local_grads(): lax.map(stats_head, (query_split, grad_split, key_split, value_split, slo...]
    all_gather x3 -> x0, blocking collectives: 40.7 us -> none  [joined(): everything = jax.tree.map(lambda part: lax.all_gather(part, axis), value)]
    gather x64 -> x0, local copies, waits for them, and re-layouts: 38.2 us -> none  [the longest x32 19.1 us: block_scores(): key_blocks = key_head[picks]]
    scatter-add x32 -> x0, other arithmetic: 32.9 us -> none  [the longest x16 16.5 us: grads_group(): key_total = carry[0].at[flat_picks].add(jnp.where(flat_live, key_terms.re...]
  transfers between devices with their start and end apart: 7 -> 0, of which waited for: 7 -> 0; matrix products, arithmetic and copies ran while one was open for 6% -> 0% of each run, Pallas kernels for 0% -> 0%
where the time goes in v2:
time: 145 us
  Pallas kernels  136 us (94%)
  local copies, waits for them, and re-layouts  7.46 us (5%)
    pallas_call x1, Pallas kernels, head_shards(): pl.pallas_call(functools.partial(to_heads_kernel, devices, half), out_sha...  64.4 us
    pallas_call x1, Pallas kernels, head_shards(): pl.pallas_call(functools.partial(from_heads_kernel, devices, half), out_s...  50.8 us
    pallas_call x1, Pallas kernels, head_shards(): pl.pallas_call(grads_kernel, out_shape=(like(all_rows, width), like(half_...  10.8 us
    unnamed x11, local copies, waits for them, and re-layouts  7.26 us
    pallas_call x1, Pallas kernels, head_shards(): pl.pallas_call(functools.partial(combine_kernel, half), out_shape=like(2,...  5.07 us
    pallas_call x1, Pallas kernels, head_shards(): pl.pallas_call(stats_kernel, out_shape=like(3, stat_rows, BLOCK, dtype=jn...  4.97 us

profile of v2, /device:TPU:0, one launch (start us, length us, event | category | flops | bytes accessed | tf_op | source)
XLA Modules:
  0.0 144.8 jit_solution(13520899680524382110)
XLA Ops:
  0.7 0.7 dynamic-slice_subtract_fusion
  1.3 0.1 copy.9
  1.4 0.1 sub.15.picks
  1.5 0.0 copy-start
  1.6 1.2 copy-done
  2.8 0.0 copy-start.1
  2.8 1.2 copy-done.1
  4.0 0.0 copy-start.2
  4.0 1.0 copy-done.2
  5.0 0.0 copy-start.3
  5.0 1.0 copy-done.3
  6.1 64.4 %to_heads.1 = (bf16[2048,256]{1,0:T(8,128)(2,1)S(1)}, bf16[2048,256]{1,0:T(8,128)(2,1)S(1)}, bf16[2048,256]{1,0:T(8,128)(2,1)S(1)}, bf16[2048,256]{1,0:T(8,128)(2,1)S(1)}) custom-call(bf16[128,2048]{1,0:T(8,128)(2,1)S(1)} %copy-done.2, bf16[128,2048]{1,0:T(8,128)(2,1)S(1)} %copy-done.3, bf16[1024,512]{1,0:T(8,128)(2,1)S(1)} %copy-done, ...), custom_call_target="tpu_custom_call" | custom-call | tf_op jit(solution)/shard_map/to_heads/pallas_call | solution.py:499
  70.5 5.0 %stats.1.stats_ref = f32[3,32,128]{2,1,0:T(8,128)S(1)} custom-call(s32[64]{0:T(128)S(1)} %sub.15.picks, bf16[2048,256]{1,0:T(8,128)(2,1)S(1)} %get-tuple-element.10.query_ref, bf16[2048,256]{1,0:T(8,128)(2,1)S(1)} %get-tuple-element.11.grad_ref, bf16[2048,256]{1,0:T(8,128)(2,1)S(1)} %get-tuple-element.12.key_ref, ...), custom_call_target="tpu_custom_call" | custom-call | tf_op jit(solution)/shard_map/stats/pallas_call | solution.py:515
  75.5 5.1 %combine.1.stats_ref = f32[2,32,128]{2,1,0:T(8,128)S(1)} custom-call(f32[3,32,128]{2,1,0:T(8,128)S(1)} %stats.1.stats_ref), custom_call_target="tpu_custom_call" | custom-call | tf_op jit(solution)/shard_map/combine/pallas_call | solution.py:527
  80.5 10.8 %head_grads.1 = (bf16[2048,256]{1,0:T(8,128)(2,1)S(1)}, bf16[2048,256]{1,0:T(8,128)(2,1)S(1)}, bf16[2048,256]{1,0:T(8,128)(2,1)S(1)}) custom-call(s32[64]{0:T(128)S(1)} %sub.15.picks, f32[2,32,128]{2,1,0:T(8,128)S(1)} %combine.1.stats_ref, bf16[2048,256]{1,0:T(8,128)(2,1)S(1)} %get-tuple-element.10.query_ref, ...), custom_call_target="tpu_custom_call" | custom-call | tf_op jit(solution)/shard_map/head_grads/pallas_call | solution.py:540
  91.3 50.8 %from_heads.1 = (bf16[128,2048]{1,0:T(8,128)(2,1)S(1)}, bf16[1024,512]{1,0:T(8,128)(2,1)S(1)}, bf16[1024,512]{1,0:T(8,128)(2,1)S(1)}) custom-call(bf16[2048,256]{1,0:T(8,128)(2,1)S(1)} %get-tuple-element.14.query_ref, bf16[2048,256]{1,0:T(8,128)(2,1)S(1)} %get-tuple-element.15.key_ref, bf16[2048,256]{1,0:T(8,128)(2,1)S(1)} %get-tuple-element.16.value_ref), custom_call_target="tpu_custom_call" | custom-call | tf_op jit(solution)/shard_map/from_heads/pallas_call | solution.py:554
  142.1 0.8 copy.13
  142.9 1.0 copy.14
  143.8 1.0 copy.15
Async XLA Ops:
  1.5 1.2 copy-start
  2.8 1.2 copy-start.1
  4.0 1.0 copy-start.2
  5.0 1.0 copy-start.3

commit v3 on v0

--- a/solution.py
+++ b/solution.py
@@ -1,8 +1,11 @@
+import functools
 import math
 
 import jax
 import jax.numpy as jnp
 from jax import lax
+from jax.experimental import pallas as pl
+from jax.experimental.pallas import tpu as pltpu
 from jax.sharding import PartitionSpec as P
 
 HEAD_DIM = 128
@@ -172,7 +175,7 @@
     return (query_grad, key_grad, value_grad)
 
 
-def shards(queries, keys, values, grad_out, blocks):
+def span_shards(queries, keys, values, grad_out, blocks):
     query_span, grad_span = (
         lax.all_gather(queries, "memory", axis=0, tiled=True),
         lax.all_gather(grad_out, "memory", axis=0, tiled=True),
@@ -196,6 +199,312 @@
         query_part.astype(jnp.bfloat16), "memory", scatter_dimension=0, tiled=True
     )
     return (grad_query, key_grad.astype(jnp.bfloat16), value_grad.astype(jnp.bfloat16))
+
+
+MESH = pl.DeviceIdType.MESH
+NT = (((1,), (1,)), ((), ()))
+TN = (((0,), (0,)), ((), ()))
+UNROLL = 2
+
+
+def position():
+    memory_size = lax.axis_size("memory")
+    here = lax.axis_index("query") * memory_size + lax.axis_index("memory")
+    return lax.axis_index("group"), here, memory_size
+
+
+def meet(group, here, devices, memory_size):
+    barrier = pltpu.get_barrier_semaphore()
+    for step in range(1, devices):
+        peer = lax.rem(here + step, devices)
+        pl.semaphore_signal(
+            barrier,
+            inc=1,
+            device_id=(group, peer // memory_size, lax.rem(peer, memory_size)),
+            device_id_type=MESH,
+        )
+    pl.semaphore_wait(barrier, devices - 1)
+
+
+def columns(index, width):
+    return pl.ds(pl.multiple_of(index * width, width), width)
+
+
+def rows(index, size):
+    return pl.ds(pl.multiple_of(index * size, size), size)
+
+
+def away(group, memory_size, peer):
+    return (group, peer // memory_size, lax.rem(peer, memory_size))
+
+
+def fused_kernel(
+    devices, half, heads,
+    picks, earlier, latest, live_ref, query_ref, grad_ref, key_ref, value_ref,
+    query_out, key_out, value_out,
+    query_in, grad_in, key_in, value_in, weights, products, stats, other, key_sums, value_sums,
+    query_stage, key_stage, value_stage, parts,
+    in_send, in_recv, in_own, stat_send, stat_recv, out_send, out_recv, out_own,
+):
+    scale = 1.0 / math.sqrt(HEAD_DIM)
+    group, here, memory_size = position()
+    my_query, my_memory = here // memory_size, lax.rem(here, memory_size)
+    side, lane = my_memory // half, lax.rem(my_memory, half)
+    partner = (group, my_query, lax.rem(my_memory + half, memory_size))
+    row_count, own_blocks = query_ref.shape[0], key_ref.shape[0]
+    memory_rows = own_blocks * BLOCK
+    query_blocks = query_in.shape[1] // BLOCK
+    half_blocks = key_in[0].shape[0]
+    slots = 2 * query_blocks
+    meet(group, here, devices, memory_size)
+
+    def transfer(source, target, step, device, send, recv, own):
+        if step == 0:
+            return pltpu.make_async_copy(source, target, own)
+        return pltpu.make_async_remote_copy(
+            src_ref=source, dst_ref=target, send_sem=send, recv_sem=recv,
+            device_id=device, device_id_type=MESH,
+        )
+
+    arrivals = []
+    for head in range(heads):
+        copies = []
+        for which, (source, target) in enumerate(((key_ref, key_in), (value_ref, value_in))):
+            for step in range(half):
+                peer = lax.rem(lane + step, half)
+                at = 2 * devices + which * half + step
+                copies.append(transfer(
+                    source.at[:, :, columns(peer * heads + head, HEAD_DIM)],
+                    target[head].at[pl.ds(lane * own_blocks, own_blocks)],
+                    step, (group, my_query, side * half + peer),
+                    in_send.at[head, at], in_recv.at[head, at], in_own.at[head, which],
+                ))
+        for step in range(devices):
+            peer = lax.rem(here + step, devices)
+            first = (peer // memory_size * half + lax.rem(lax.rem(peer, memory_size), half)) * heads
+            for which, (source, target) in enumerate(((query_ref, query_in), (grad_ref, grad_in))):
+                at = which * devices + step
+                copies.append(transfer(
+                    source.at[:, columns(first + head, HEAD_DIM)],
+                    target.at[head, rows(here, row_count), :],
+                    step, away(group, memory_size, peer),
+                    in_send.at[head, at], in_recv.at[head, at], in_own.at[head, 2 + which],
+                ))
+        for copy in copies:
+            copy.start()
+        arrivals.append(copies)
+
+    key_sums[0] = jnp.zeros(key_sums.shape[1:], jnp.float32)
+    value_sums[0] = jnp.zeros(value_sums.shape[1:], jnp.float32)
+    returns = []
+    for head in range(heads):
+        for copy in arrivals[head]:
+            copy.wait()
+
+        def pick(block, slot):
+            number = head * slots + 2 * block + slot
+            return picks[number], live_ref[pl.ds(number, 1), :]
+
+        def stats_step(block, carry):
+            mine = rows(block, BLOCK)
+            query, grad = query_in[head, mine, :], grad_in[head, mine, :]
+            scores = []
+            for slot in range(2):
+                place, live = pick(block, slot)
+                score = lax.dot_general(
+                    key_in[head][place], query, NT, preferred_element_type=jnp.float32
+                )
+                scores.append(jnp.where(live > 0.0, score * scale, -1e30))
+                products[2 * block + slot] = lax.dot_general(
+                    value_in[head][place], grad, NT, preferred_element_type=jnp.float32
+                )
+            top = jnp.maximum(
+                jnp.max(scores[0], axis=0, keepdims=True), jnp.max(scores[1], axis=0, keepdims=True)
+            )
+            total, weighted = 0.0, 0.0
+            for slot in range(2):
+                place, live = pick(block, slot)
+                weight = jnp.exp(scores[slot] - top) * live
+                weights[2 * block + slot] = weight
+                total += jnp.sum(weight, axis=0, keepdims=True)
+                weighted += jnp.sum(weight * products[2 * block + slot], axis=0, keepdims=True)
+            line = pl.ds(block, 1)
+            stats[head, 0, line, :] = top
+            stats[head, 1, line, :] = total
+            stats[head, 2, line, :] = weighted
+            return carry
+
+        lax.fori_loop(0, query_blocks, stats_step, 0, unroll=UNROLL)
+        exchange = pltpu.make_async_remote_copy(
+            src_ref=stats.at[head], dst_ref=other.at[head],
+            send_sem=stat_send.at[head], recv_sem=stat_recv.at[head],
+            device_id=partner, device_id_type=MESH,
+        )
+        exchange.start()
+        exchange.wait()
+        ours = (stats[head, 0], stats[head, 1], stats[head, 2])
+        top, total, weighted = combine_stats(ours, (other[head, 0], other[head, 1], other[head, 2]))
+        stats[head, 0] = jnp.exp(ours[0] - top) / total
+        stats[head, 1] = weighted / total
+
+        def grads_step(block, carry):
+            mine, line = rows(block, BLOCK), pl.ds(block, 1)
+            query, grad = query_in[head, mine, :], grad_in[head, mine, :]
+            factor, delta = stats[head, 0, line, :], stats[head, 1, line, :]
+            query_term = 0.0
+            plain = (((1,), (0,)), ((), ()))
+            key_terms, value_terms = [], []
+            for slot in range(2):
+                place, live = pick(block, slot)
+                number = 2 * block + slot
+                probs = weights[number] * factor
+                score_grad = (probs * (products[number] - delta)).astype(jnp.bfloat16)
+                value_terms.append(lax.dot_general(
+                    probs.astype(jnp.bfloat16), grad, plain, preferred_element_type=jnp.float32
+                ))
+                key_terms.append(lax.dot_general(
+                    score_grad, query, plain, preferred_element_type=jnp.float32
+                ))
+                query_term += lax.dot_general(
+                    score_grad, key_in[head][place], TN, preferred_element_type=jnp.float32
+                )
+            query_stage[head, mine, :] = (query_term * scale).astype(query_stage.dtype)
+            for slot in range(2):
+                number = 2 * block + slot
+                before = earlier[head * slots + number]
+                key_sums[number + 1] = key_sums[before] + key_terms[slot]
+                value_sums[number + 1] = value_sums[before] + value_terms[slot]
+            return carry
+
+        lax.fori_loop(0, query_blocks, grads_step, 0, unroll=UNROLL)
+
+        def finish_step(block, carry):
+            last = latest[head * half_blocks + block]
+            mine = rows(block, BLOCK)
+            key_stage[head, mine, :] = (key_sums[last] * scale).astype(key_stage.dtype)
+            value_stage[head, mine, :] = value_sums[last].astype(value_stage.dtype)
+            return carry
+
+        lax.fori_loop(0, half_blocks, finish_step, 0, unroll=UNROLL)
+
+        copies = []
+        for which, (source, target) in enumerate(((key_stage, key_out), (value_stage, value_out))):
+            for step in range(half):
+                peer = lax.rem(lane + step, half)
+                at = devices + which * half + step
+                copies.append(transfer(
+                    source.at[head, rows(peer, memory_rows), :],
+                    target.at[:, columns(lane * heads + head, HEAD_DIM)],
+                    step, (group, my_query, side * half + peer),
+                    out_send.at[head, at], out_recv.at[head, at], out_own.at[head, which],
+                ))
+        for step in range(devices):
+            peer = lax.rem(here + step, devices)
+            copies.append(transfer(
+                query_stage.at[head, rows(peer, row_count), :],
+                parts.at[side, :, columns((my_query * half + lane) * heads + head, HEAD_DIM)],
+                step, away(group, memory_size, peer),
+                out_send.at[head, step], out_recv.at[head, step], out_own.at[head, 2],
+            ))
+        for copy in copies:
+            copy.start()
+        returns += copies
+
+    for copy in returns:
+        copy.wait()
+    query_out[...] = (parts[0].astype(jnp.float32) + parts[1].astype(jnp.float32)).astype(
+        query_out.dtype
+    )
+
+
+def head_shards(queries, keys, values, grad_out, blocks):
+    memory_size = lax.axis_size("memory")
+    devices = lax.axis_size("query") * memory_size
+    half = memory_size // 2
+    row_count, memory_rows = queries.shape[0], keys.shape[0]
+    all_rows, half_rows = row_count * devices, memory_rows * half
+    heads = keys.shape[1] // half // HEAD_DIM
+    query_blocks, half_blocks = all_rows // BLOCK, half_rows // BLOCK
+    slots = 2 * query_blocks
+    anywhere, vmem = pl.BlockSpec(memory_space=pl.ANY), pl.BlockSpec(memory_space=pltpu.VMEM)
+    smem = pl.BlockSpec(memory_space=pltpu.SMEM)
+
+    my_query, my_memory = lax.axis_index("query"), lax.axis_index("memory")
+    first_head = (my_query * half + my_memory % half) * heads
+    picks = lax.dynamic_slice_in_dim(blocks, first_head, heads, 0).reshape(heads, slots)
+    picks = picks - my_memory // half * half_blocks
+    inside = (picks >= 0) & (picks < half_blocks)
+    live = jnp.broadcast_to(inside.reshape(-1, 1), (heads * slots, BLOCK)).astype(jnp.float32)
+    numbers = jnp.arange(slots, dtype=jnp.int32)
+    same = (picks[:, :, None] == picks[:, None, :]) & (numbers[:, None] > numbers[None, :])
+    earlier = jnp.max(jnp.where(same, numbers + 1, 0), axis=2)
+    named = picks[:, None, :] == jnp.arange(half_blocks, dtype=jnp.int32)[:, None]
+    latest = jnp.max(jnp.where(named, numbers + 1, 0), axis=2)
+
+    places = jnp.clip(picks, 0, half_blocks - 1)
+
+    def blocked(array):
+        return array.reshape(-1, BLOCK, array.shape[1])
+
+    def half_precision(*shape):
+        return pltpu.VMEM(shape, jnp.bfloat16)
+
+    def single_precision(*shape):
+        return pltpu.VMEM(shape, jnp.float32)
+
+    def semaphores(*shape):
+        return pltpu.SemaphoreType.DMA(shape)
+
+    arrivals, returns = 2 * devices + 2 * half, devices + 2 * half
+    return pl.pallas_call(
+        functools.partial(fused_kernel, devices, half, heads),
+        out_shape=(
+            jax.ShapeDtypeStruct(queries.shape, jnp.bfloat16),
+            jax.ShapeDtypeStruct(keys.shape, jnp.bfloat16),
+            jax.ShapeDtypeStruct(values.shape, jnp.bfloat16),
+        ),
+        in_specs=[smem] * 3 + [vmem] + [anywhere] * 4,
+        out_specs=(vmem, anywhere, anywhere),
+        scratch_shapes=[
+            half_precision(heads, all_rows, HEAD_DIM),
+            half_precision(heads, all_rows, HEAD_DIM),
+            [half_precision(half_blocks, BLOCK, HEAD_DIM)] * heads,
+            [half_precision(half_blocks, BLOCK, HEAD_DIM)] * heads,
+            single_precision(slots, BLOCK, BLOCK),
+            single_precision(slots, BLOCK, BLOCK),
+            single_precision(heads, 3, query_blocks, BLOCK),
+            single_precision(heads, 3, query_blocks, BLOCK),
+            single_precision(slots + 1, BLOCK, HEAD_DIM),
+            single_precision(slots + 1, BLOCK, HEAD_DIM),
+            half_precision(heads, all_rows, HEAD_DIM),
+            half_precision(heads, half_rows, HEAD_DIM),
+            half_precision(heads, half_rows, HEAD_DIM),
+            half_precision(2, row_count, queries.shape[1]),
+            semaphores(heads, arrivals),
+            semaphores(heads, arrivals),
+            semaphores(heads, 4),
+            semaphores(heads),
+            semaphores(heads),
+            semaphores(heads, returns),
+            semaphores(heads, returns),
+            semaphores(heads, 3),
+        ],
+        compiler_params=pltpu.CompilerParams(
+            collective_id=0, has_side_effects=True, vmem_limit_bytes=48 * 1024 * 1024
+        ),
+        name="head_grads",
+    )(
+        places.reshape(-1), earlier.reshape(-1), latest.reshape(-1),
+        live, queries, grad_out, blocked(keys), blocked(values),
+    )
+
+
+def shards(queries, keys, values, grad_out, blocks):
+    memory_size = lax.axis_size("memory")
+    whole_heads = keys.shape[1] % (memory_size // 2 * HEAD_DIM) == 0
+    if memory_size % 2 == 0 and whole_heads and blocks.shape[2] == 2:
+        return head_shards(queries, keys, values, grad_out, blocks)
+    return span_shards(queries, keys, values, grad_out, blocks)
 
 
 def solution(mesh):

time: 725 us -> 123 us (0.17)
  waiting for transfers between devices: 318 us -> 0 us
  local copies, waits for them, and re-layouts: 175 us -> 8.08 us
  matrix products: 126 us -> 0 us
  Pallas kernels: 0 us -> 113 us
  other arithmetic: 44.4 us -> 1.01 us
  blocking collectives: 40.7 us -> 0 us
  between operations: 14.3 us -> 0.69 us
    reduce_scatter x3 -> x0, waiting for transfers between devices: 167 us -> none  [the longest x1 71.7 us: shards(): lax.psum_scatter(key_full, 'query', scatter_dimension=1, tiled=True)]
    all_gather x4 -> x0, waiting for transfers between devices: 149 us -> none  [the longest x1 47.6 us: shards(): lax.all_gather(queries, 'memory', axis=0, tiled=True)]
    dot_general x112 -> x0, matrix products: 126 us -> none  [the longest x32 37.2 us: block_scores(): jnp.einsum('gbd,gskd->gbsk', query_group, key_blocks, preferred_element_t...]
    pallas_call x0 -> x1, Pallas kernels: none -> 113 us  [head_shards(): pl.pallas_call(functools.partial(fused_kernel, devices, half, heads), out...]
    squeeze x48 -> x0, local copies, waits for them, and re-layouts: 48.2 us -> none  [local_grads(): lax.map(stats_head, (query_split, grad_split, key_split, value_split, slo...]
    all_gather x3 -> x0, blocking collectives: 40.7 us -> none  [joined(): everything = jax.tree.map(lambda part: lax.all_gather(part, axis), value)]
    gather x64 -> x0, local copies, waits for them, and re-layouts: 38.2 us -> none  [the longest x32 19.1 us: block_scores(): key_blocks = key_head[picks]]
    scatter-add x32 -> x0, other arithmetic: 32.9 us -> none  [the longest x16 16.5 us: grads_group(): key_total = carry[0].at[flat_picks].add(jnp.where(flat_live, key_terms.re...]
  transfers between devices with their start and end apart: 7 -> 0, of which waited for: 7 -> 0; matrix products, arithmetic and copies ran while one was open for 6% -> 0% of each run, Pallas kernels for 0% -> 0%
where the time goes in v3:
time: 123 us; the launch traced here: 122 us
  Pallas kernels  113 us (92%)
  local copies, waits for them, and re-layouts  8.08 us (7%)
    pallas_call x1, Pallas kernels, head_shards(): pl.pallas_call(functools.partial(fused_kernel, devices, half, heads), out...  113 us
    unnamed x11, local copies, waits for them, and re-layouts  7.28 us

profile of v3, /device:TPU:0, one launch (start us, length us, event | category | flops | bytes accessed | tf_op | source)
XLA Modules:
  0.0 122.3 jit_solution(7460583263138099017)
XLA Ops:
  0.7 0.7 and_convert_fusion
  1.4 0.1 copy.15
  1.5 0.1 sub.30
  1.6 0.2 select_reduce_fusion
  1.7 0.1 select_reduce_fusion.1
  1.9 0.1 reshape.67.latest
  1.9 0.1 reshape.66.earlier
  2.0 0.1 copy.14
  2.1 0.1 min.12.picks
  2.2 0.1 copy.16
  2.3 0.1 reshape.70
  2.4 0.1 broadcast_in_dim.31.live_ref
  2.5 0.0 copy-start
  2.5 1.2 %copy-done = bf16[1024,512]{1,0:T(8,128)(2,1)S(1)} copy-done((bf16[1024,512]{1,0:T(8,128)(2,1)S(1)}, bf16[1024,512]{1,0:T(8,128)(2,1)}, u32[]{:S(2)}) %copy-start) | copy-done | bytes 1048600
  3.7 0.0 copy-start.1
  3.7 1.2 copy-done.1
  5.0 0.0 copy-start.2
  5.0 1.0 copy-done.2
  6.0 0.0 copy-start.3
  6.0 1.0 copy-done.3
  7.0 112.5 %head_grads.1 = (bf16[128,2048]{1,0:T(8,128)(2,1)S(1)}, bf16[1024,512]{1,0:T(8,128)(2,1)S(1)}, bf16[1024,512]{1,0:T(8,128)(2,1)S(1)}) custom-call(s32[64]{0:T(128)S(1)} %min.12.picks, s32[64]{0:T(128)S(1)} %reshape.66.earlier, s32[32]{0:T(128)S(1)} %reshape.67.latest, f32[64,128]{1,0:T(8,128)S(1)} %broadcast_in_dim.31.live_ref, ...), custom_call_target="tpu_custom_call" | custom-call | tf_op jit(solution)/shard_map/head_grads/pallas_call | solution.py:459
  119.6 0.8 copy.20
  120.4 1.0 copy.21
  121.4 1.0 copy.22
  (3 shorter events, 0.0 us)
Async XLA Ops:
  2.5 1.2 %copy-start = (bf16[1024,512]{1,0:T(8,128)(2,1)S(1)}, bf16[1024,512]{1,0:T(8,128)(2,1)}, u32[]{:S(2)}) copy-start(bf16[1024,512]{1,0:T(8,128)(2,1)} %param.6) | copy-start | bytes 3145732
  3.7 1.2 %copy-start.1 = (bf16[1024,512]{1,0:T(8,128)(2,1)S(1)}, bf16[1024,512]{1,0:T(8,128)(2,1)}, u32[]{:S(2)}) copy-start(bf16[1024,512]{1,0:T(8,128)(2,1)} %param.7) | copy-start | bytes 3145732
  5.0 1.0 copy-start.2
  6.0 1.0 copy-start.3

commit v4 on v3

--- a/solution.py
+++ b/solution.py
@@ -296,10 +296,12 @@
 
     key_sums[0] = jnp.zeros(key_sums.shape[1:], jnp.float32)
     value_sums[0] = jnp.zeros(value_sums.shape[1:], jnp.float32)
-    returns = []
+    returns, pending = [], []
     for head in range(heads):
         for copy in arrivals[head]:
             copy.wait()
+        for copy in pending:
+            copy.start()
 
         def pick(block, slot):
             number = head * slots + 2 * block + slot
@@ -406,10 +408,11 @@
                 step, away(group, memory_size, peer),
                 out_send.at[head, step], out_recv.at[head, step], out_own.at[head, 2],
             ))
-        for copy in copies:
-            copy.start()
         returns += copies
-
+        pending = copies
+
+    for copy in pending:
+        copy.start()
     for copy in returns:
         copy.wait()
     query_out[...] = (parts[0].astype(jnp.float32) + parts[1].astype(jnp.float32)).astype(
@@ -490,7 +493,7 @@
             semaphores(heads, 3),
         ],
         compiler_params=pltpu.CompilerParams(
-            collective_id=0, has_side_effects=True, vmem_limit_bytes=48 * 1024 * 1024
+            collective_id=0, has_side_effects=True, vmem_limit_bytes=62 * 1024 * 1024
         ),
         name="head_grads",
     )(

time: 123 us -> 125 us (1.016)
  Pallas kernels: 113 us -> 115 us
    pallas_call x1, Pallas kernels: 113 us -> 115 us  [head_shards(): pl.pallas_call(functools.partial(fused_kernel, devices, half, heads), out...]
    unnamed x11 -> x7, local copies, waits for them, and re-layouts: 7.28 us -> 4.55 us
where the time goes in v4:
time: 125 us
  Pallas kernels  115 us (92%)
  local copies, waits for them, and re-layouts  7.51 us (6%)
    pallas_call x1, Pallas kernels, head_shards(): pl.pallas_call(functools.partial(fused_kernel, devices, half, heads), out...  115 us
    unnamed x7, local copies, waits for them, and re-layouts  4.55 us

profile of v4, /device:TPU:0, one launch (start us, length us, event | category | flops | bytes accessed | tf_op | source)
XLA Modules:
  0.0 124.5 jit_solution(17697665784692844495)
XLA Ops:
  0.7 0.7 and_convert_fusion
  1.4 0.1 copy.15
  1.5 0.1 sub.30
  1.6 0.2 select_reduce_fusion
  1.7 0.1 select_reduce_fusion.1
  1.9 0.6 reshape.67.latest
  2.5 0.6 reshape.66.earlier
  3.1 0.1 copy.14
  3.1 0.6 min.12.picks
  3.8 0.1 copy.16
  3.9 0.1 reshape.70
  4.0 0.7 broadcast_in_dim.31.live_ref
  4.7 115.3 %head_grads.1 = (bf16[128,2048]{1,0:T(8,128)(2,1)}, bf16[1024,512]{1,0:T(8,128)(2,1)}, bf16[1024,512]{1,0:T(8,128)(2,1)}) custom-call(s32[64]{0:T(128)} %min.12.picks, s32[64]{0:T(128)} %reshape.66.earlier, s32[32]{0:T(128)} %reshape.67.latest, f32[64,128]{1,0:T(8,128)} %broadcast_in_dim.31.live_ref, bf16[128,2048]{1,0:T(8,128)(2,1)} %query_ref.1, ...), custom_call_target="tpu_custom_call" | custom-call | tf_op jit(solution)/shard_map/head_grads/pallas_call | solution.py:462
  120.0 0.0 copy-start.1
  120.0 2.0 %copy.20 = bf16[128,2048]{1,0:T(8,128)(2,1)} copy(bf16[128,2048]{1,0:T(8,128)(2,1)} %get-tuple-element.8) | data formatting | bytes 1048576
  121.9 0.0 copy-done.1
  121.9 0.0 copy-start
  121.9 1.0 copy.21
  122.9 0.6 copy-done
  123.5 1.0 copy.22
  (3 shorter events, 0.0 us)
Async XLA Ops:
  120.0 2.0 %copy-start.1 = (bf16[1024,512]{1,0:T(8,128)(2,1)S(1)}, bf16[1024,512]{1,0:T(8,128)(2,1)}, u32[]{:S(2)}) copy-start(bf16[1024,512]{1,0:T(8,128)(2,1)} %get-tuple-element.9) | copy-start | bytes 3145732
  121.9 1.6 %copy-start = (bf16[1024,512]{1,0:T(8,128)(2,1)S(1)}, bf16[1024,512]{1,0:T(8,128)(2,1)}, u32[]{:S(2)}) copy-start(bf16[1024,512]{1,0:T(8,128)(2,1)} %get-tuple-element.10) | copy-start | bytes 3145732

commit v5 on v3

--- a/solution.py
+++ b/solution.py
@@ -240,10 +240,10 @@
 
 def fused_kernel(
     devices, half, heads,
-    picks, earlier, latest, live_ref, query_ref, grad_ref, key_ref, value_ref,
-    query_out, key_out, value_out,
+    table, query_ref, grad_ref, key_ref, value_ref,
+    parts, key_out, value_out,
     query_in, grad_in, key_in, value_in, weights, products, stats, other, key_sums, value_sums,
-    query_stage, key_stage, value_stage, parts,
+    query_stage, key_stage, value_stage,
     in_send, in_recv, in_own, stat_send, stat_recv, out_send, out_recv, out_own,
 ):
     scale = 1.0 / math.sqrt(HEAD_DIM)
@@ -256,6 +256,7 @@
     query_blocks = query_in.shape[1] // BLOCK
     half_blocks = key_in[0].shape[0]
     slots = 2 * query_blocks
+    lines = 2 * slots + half_blocks
     meet(group, here, devices, memory_size)
 
     def transfer(source, target, step, device, send, recv, own):
@@ -302,8 +303,8 @@
             copy.wait()
 
         def pick(block, slot):
-            number = head * slots + 2 * block + slot
-            return picks[number], live_ref[pl.ds(number, 1), :]
+            coded = table[head * lines + slots + half_blocks + 2 * block + slot]
+            return jnp.maximum(coded - 1, 0), jnp.minimum(coded, 1).astype(jnp.float32)
 
         def stats_step(block, carry):
             mine = rows(block, BLOCK)
@@ -314,7 +315,7 @@
                 score = lax.dot_general(
                     key_in[head][place], query, NT, preferred_element_type=jnp.float32
                 )
-                scores.append(jnp.where(live > 0.0, score * scale, -1e30))
+                scores.append(score * (scale * live) + (live - 1.0) * 1e30)
                 products[2 * block + slot] = lax.dot_general(
                     value_in[head][place], grad, NT, preferred_element_type=jnp.float32
                 )
@@ -371,7 +372,7 @@
             query_stage[head, mine, :] = (query_term * scale).astype(query_stage.dtype)
             for slot in range(2):
                 number = 2 * block + slot
-                before = earlier[head * slots + number]
+                before = table[head * lines + number]
                 key_sums[number + 1] = key_sums[before] + key_terms[slot]
                 value_sums[number + 1] = value_sums[before] + value_terms[slot]
             return carry
@@ -379,7 +380,7 @@
         lax.fori_loop(0, query_blocks, grads_step, 0, unroll=UNROLL)
 
         def finish_step(block, carry):
-            last = latest[head * half_blocks + block]
+            last = table[head * lines + slots + block]
             mine = rows(block, BLOCK)
             key_stage[head, mine, :] = (key_sums[last] * scale).astype(key_stage.dtype)
             value_stage[head, mine, :] = value_sums[last].astype(value_stage.dtype)
@@ -412,9 +413,6 @@
 
     for copy in returns:
         copy.wait()
-    query_out[...] = (parts[0].astype(jnp.float32) + parts[1].astype(jnp.float32)).astype(
-        query_out.dtype
-    )
 
 
 def head_shards(queries, keys, values, grad_out, blocks):
@@ -426,7 +424,7 @@
     heads = keys.shape[1] // half // HEAD_DIM
     query_blocks, half_blocks = all_rows // BLOCK, half_rows // BLOCK
     slots = 2 * query_blocks
-    anywhere, vmem = pl.BlockSpec(memory_space=pl.ANY), pl.BlockSpec(memory_space=pltpu.VMEM)
+    anywhere = pl.BlockSpec(memory_space=pl.ANY)
     smem = pl.BlockSpec(memory_space=pltpu.SMEM)
 
     my_query, my_memory = lax.axis_index("query"), lax.axis_index("memory")
@@ -434,14 +432,20 @@
     picks = lax.dynamic_slice_in_dim(blocks, first_head, heads, 0).reshape(heads, slots)
     picks = picks - my_memory // half * half_blocks
     inside = (picks >= 0) & (picks < half_blocks)
-    live = jnp.broadcast_to(inside.reshape(-1, 1), (heads * slots, BLOCK)).astype(jnp.float32)
-    numbers = jnp.arange(slots, dtype=jnp.int32)
-    same = (picks[:, :, None] == picks[:, None, :]) & (numbers[:, None] > numbers[None, :])
-    earlier = jnp.max(jnp.where(same, numbers + 1, 0), axis=2)
-    named = picks[:, None, :] == jnp.arange(half_blocks, dtype=jnp.int32)[:, None]
-    latest = jnp.max(jnp.where(named, numbers + 1, 0), axis=2)
-
-    places = jnp.clip(picks, 0, half_blocks - 1)
+    coded = jnp.where(inside, picks + 1, 0)
+    line = jnp.arange(2 * slots + half_blocks, dtype=jnp.int32)[:, None]
+    number = jnp.arange(slots, dtype=jnp.int32)[None, :]
+    ids = jnp.broadcast_to(jnp.arange(half_blocks, dtype=jnp.int32), (heads, half_blocks))
+    wanted = jnp.concatenate([picks, ids, picks], axis=1)[:, :, None]
+    first_part = line < slots + half_blocks
+    chosen = jnp.where(
+        first_part,
+        (wanted == picks[:, None, :]) & ((line >= slots) | (number < line)),
+        line - slots - half_blocks == number,
+    )
+    table = jnp.max(
+        jnp.where(chosen, jnp.where(first_part, number + 1, coded[:, None, :]), 0), axis=2
+    ).reshape(-1)
 
     def blocked(array):
         return array.reshape(-1, BLOCK, array.shape[1])
@@ -456,15 +460,15 @@
         return pltpu.SemaphoreType.DMA(shape)
 
     arrivals, returns = 2 * devices + 2 * half, devices + 2 * half
-    return pl.pallas_call(
+    parts, key_grad, value_grad = pl.pallas_call(
         functools.partial(fused_kernel, devices, half, heads),
         out_shape=(
-            jax.ShapeDtypeStruct(queries.shape, jnp.bfloat16),
+            jax.ShapeDtypeStruct((2, *queries.shape), jnp.bfloat16),
             jax.ShapeDtypeStruct(keys.shape, jnp.bfloat16),
             jax.ShapeDtypeStruct(values.shape, jnp.bfloat16),
         ),
-        in_specs=[smem] * 3 + [vmem] + [anywhere] * 4,
-        out_specs=(vmem, anywhere, anywhere),
+        in_specs=[smem] + [anywhere] * 4,
+        out_specs=(anywhere,) * 3,
         scratch_shapes=[
             half_precision(heads, all_rows, HEAD_DIM),
             half_precision(heads, all_rows, HEAD_DIM),
@@ -479,7 +483,6 @@
             half_precision(heads, all_rows, HEAD_DIM),
             half_precision(heads, half_rows, HEAD_DIM),
             half_precision(heads, half_rows, HEAD_DIM),
-            half_precision(2, row_count, queries.shape[1]),
             semaphores(heads, arrivals),
             semaphores(heads, arrivals),
             semaphores(heads, 4),
@@ -490,13 +493,13 @@
             semaphores(heads, 3),
         ],
         compiler_params=pltpu.CompilerParams(
-            collective_id=0, has_side_effects=True, vmem_limit_bytes=48 * 1024 * 1024
+            collective_id=0, has_side_effects=True, vmem_limit_bytes=62 * 1024 * 1024
         ),
         name="head_grads",
-    )(
-        places.reshape(-1), earlier.reshape(-1), latest.reshape(-1),
-        live, queries, grad_out, blocked(keys), blocked(values),
-    )
+    )(table, queries, grad_out, blocked(keys), blocked(values))
+
+    query_grad = parts[0].astype(jnp.float32) + parts[1].astype(jnp.float32)
+    return (query_grad.astype(jnp.bfloat16), key_grad, value_grad)
 
 
 def shards(queries, keys, values, grad_out, blocks):

time: 123 us -> 120 us (0.976)
  local copies, waits for them, and re-layouts: 8.08 us -> 3.41 us
  other arithmetic: 1.01 us -> 3.12 us
    unnamed x11 -> x6, local copies, waits for them, and re-layouts: 7.28 us -> 2.58 us
    convert_element_type x1, other arithmetic: 0.69 us -> 2.21 us  [head_shards(): return (query_grad.astype(jnp.bfloat16), key_grad, value_grad)]
where the time goes in v5:
time: 120 us
  Pallas kernels  113 us (94%)
  local copies, waits for them, and re-layouts  3.41 us (3%)
  other arithmetic  3.12 us (3%)
    pallas_call x1, Pallas kernels, head_shards(): pl.pallas_call(functools.partial(fused_kernel, devices, half, heads), out...  113 us
    unnamed x6, local copies, waits for them, and re-layouts  2.58 us

profile of v5, /device:TPU:0, one launch (start us, length us, event | category | flops | bytes accessed | tf_op | source)
XLA Modules:
  0.0 120.0 jit_solution(3537592959404029170)
XLA Ops:
  0.7 0.7 dynamic-slice_subtract_fusion
  1.4 0.1 copy.10
  1.5 0.1 sub.30
  1.6 0.1 pad_add_fusion
  1.7 0.1 select_reduce_fusion
  1.8 0.6 reshape.80.table
  2.4 112.7 %head_grads.1 = (bf16[2,128,2048]{2,1,0:T(8,128)(2,1)}, bf16[1024,512]{1,0:T(8,128)(2,1)}, bf16[1024,512]{1,0:T(8,128)(2,1)}) custom-call(s32[160]{0:T(256)} %reshape.80.table, bf16[128,2048]{1,0:T(8,128)(2,1)} %query_ref.1, bf16[128,2048]{1,0:T(8,128)(2,1)} %grad_ref.1, bf16[8,128,512]{2,1,0:T(8,128)(2,1)} %bitcast.4, bf16[8,128,512]{2,1,0:T(8,128)(2,1)} %bitcast.5), custom_call_target="tpu_custom_call" | custom-call | tf_op jit(solution)/shard_map/head_grads/pallas_call | solution.py:463
  115.2 0.0 copy-start.1
  115.2 2.2 %fusion = bf16[128,2048]{1,0:T(8,128)(2,1)} fusion(bf16[2,128,2048]{2,1,0:T(8,128)(2,1)} %get-tuple-element.6), kind=kLoop, calls=%fused_computation.1 | loop fusion | flops 1048576 | bytes 1572864 | tf_op jit(solution)/shard_map/convert_element_type | solution.py:502
  117.4 0.0 copy-done.1
  117.4 0.0 copy-start
  117.4 1.0 copy.13
  118.4 0.6 copy-done
  119.0 1.0 copy.14
  (7 shorter events, 0.0 us)
Async XLA Ops:
  115.2 2.2 %copy-start.1 = (bf16[1024,512]{1,0:T(8,128)(2,1)S(1)}, bf16[1024,512]{1,0:T(8,128)(2,1)}, u32[]{:S(2)}) copy-start(bf16[1024,512]{1,0:T(8,128)(2,1)} %get-tuple-element.15) | copy-start | bytes 3145732
  117.4 1.6 %copy-start = (bf16[1024,512]{1,0:T(8,128)(2,1)S(1)}, bf16[1024,512]{1,0:T(8,128)(2,1)}, u32[]{:S(2)}) copy-start(bf16[1024,512]{1,0:T(8,128)(2,1)} %get-tuple-element.16) | copy-start | bytes 3145732

commit v6 on v5

--- a/solution.py
+++ b/solution.py
@@ -204,7 +204,7 @@
 MESH = pl.DeviceIdType.MESH
 NT = (((1,), (1,)), ((), ()))
 TN = (((0,), (0,)), ((), ()))
-UNROLL = 2
+UNROLL = 4
 
 
 def position():
@@ -259,6 +259,14 @@
     lines = 2 * slots + half_blocks
     meet(group, here, devices, memory_size)
 
+    query_size = devices // memory_size
+    peers = []
+    for hop in (*range(memory_size // 2, 0, -1), *range(memory_size // 2 + 1, memory_size), 0):
+        for turn in range(query_size):
+            peer_query = lax.rem(my_query + turn, query_size)
+            peer_memory = lax.rem(my_memory + hop, memory_size)
+            peers.append((hop * query_size + turn, peer_query * memory_size + peer_memory))
+
     def transfer(source, target, step, device, send, recv, own):
         if step == 0:
             return pltpu.make_async_copy(source, target, own)
@@ -280,8 +288,7 @@
                     step, (group, my_query, side * half + peer),
                     in_send.at[head, at], in_recv.at[head, at], in_own.at[head, which],
                 ))
-        for step in range(devices):
-            peer = lax.rem(here + step, devices)
+        for step, peer in peers:
             first = (peer // memory_size * half + lax.rem(lax.rem(peer, memory_size), half)) * heads
             for which, (source, target) in enumerate(((query_ref, query_in), (grad_ref, grad_in))):
                 at = which * devices + step
@@ -379,6 +386,18 @@
 
         lax.fori_loop(0, query_blocks, grads_step, 0, unroll=UNROLL)
 
+        copies = []
+        for step, peer in peers:
+            copies.append(transfer(
+                query_stage.at[head, rows(peer, row_count), :],
+                parts.at[side, :, columns((my_query * half + lane) * heads + head, HEAD_DIM)],
+                step, away(group, memory_size, peer),
+                out_send.at[head, step], out_recv.at[head, step], out_own.at[head, 2],
+            ))
+        for copy in copies:
+            copy.start()
+        returns += copies
+
         def finish_step(block, carry):
             last = table[head * lines + slots + block]
             mine = rows(block, BLOCK)
@@ -399,14 +418,6 @@
                     step, (group, my_query, side * half + peer),
                     out_send.at[head, at], out_recv.at[head, at], out_own.at[head, which],
                 ))
-        for step in range(devices):
-            peer = lax.rem(here + step, devices)
-            copies.append(transfer(
-                query_stage.at[head, rows(peer, row_count), :],
-                parts.at[side, :, columns((my_query * half + lane) * heads + head, HEAD_DIM)],
-                step, away(group, memory_size, peer),
-                out_send.at[head, step], out_recv.at[head, step], out_own.at[head, 2],
-            ))
         for copy in copies:
             copy.start()
         returns += copies

time: 120 us -> 119 us (level)
  Pallas kernels: 113 us -> 111 us
    pallas_call x1, Pallas kernels: 113 us -> 111 us  [head_shards(): pl.pallas_call(functools.partial(fused_kernel, devices, half, heads), out...]
where the time goes in v6:
time: 119 us; the launch traced here: 118 us
  Pallas kernels  111 us (93%)
  local copies, waits for them, and re-layouts  3.41 us (3%)
  other arithmetic  3.12 us (3%)
    pallas_call x1, Pallas kernels, head_shards(): pl.pallas_call(functools.partial(fused_kernel, devices, half, heads), out...  111 us
    unnamed x6, local copies, waits for them, and re-layouts  2.58 us

profile of v6, /device:TPU:0, one launch (start us, length us, event | category | flops | bytes accessed | tf_op | source)
XLA Modules:
  0.0 118.3 jit_solution(18197644167283686651)
XLA Ops:
  0.7 0.7 dynamic-slice_subtract_fusion
  1.4 0.1 copy.10
  1.5 0.1 sub.30
  1.6 0.1 pad_add_fusion
  1.7 0.1 select_reduce_fusion
  1.8 0.6 reshape.80.table
  2.4 111.0 %head_grads.1 = (bf16[2,128,2048]{2,1,0:T(8,128)(2,1)}, bf16[1024,512]{1,0:T(8,128)(2,1)}, bf16[1024,512]{1,0:T(8,128)(2,1)}) custom-call(s32[160]{0:T(256)} %reshape.80.table, bf16[128,2048]{1,0:T(8,128)(2,1)} %query_ref.1, bf16[128,2048]{1,0:T(8,128)(2,1)} %grad_ref.1, bf16[8,128,512]{2,1,0:T(8,128)(2,1)} %bitcast.4, bf16[8,128,512]{2,1,0:T(8,128)(2,1)} %bitcast.5), custom_call_target="tpu_custom_call" | custom-call | tf_op jit(solution)/shard_map/head_grads/pallas_call | solution.py:474
  113.5 0.0 copy-start.1
  113.5 2.2 %fusion = bf16[128,2048]{1,0:T(8,128)(2,1)} fusion(bf16[2,128,2048]{2,1,0:T(8,128)(2,1)} %get-tuple-element.6), kind=kLoop, calls=%fused_computation.1 | loop fusion | flops 1048576 | bytes 1572864 | tf_op jit(solution)/shard_map/convert_element_type | solution.py:513
  115.7 0.0 copy-done.1
  115.7 0.0 copy-start
  115.7 1.0 copy.13
  116.7 0.6 copy-done
  117.3 1.0 copy.14
  (7 shorter events, 0.0 us)
Async XLA Ops:
  113.5 2.2 %copy-start.1 = (bf16[1024,512]{1,0:T(8,128)(2,1)S(1)}, bf16[1024,512]{1,0:T(8,128)(2,1)}, u32[]{:S(2)}) copy-start(bf16[1024,512]{1,0:T(8,128)(2,1)} %get-tuple-element.15) | copy-start | bytes 3145732
  115.7 1.6 %copy-start = (bf16[1024,512]{1,0:T(8,128)(2,1)S(1)}, bf16[1024,512]{1,0:T(8,128)(2,1)}, u32[]{:S(2)}) copy-start(bf16[1024,512]{1,0:T(8,128)(2,1)} %get-tuple-element.16) | copy-start | bytes 3145732

commit v7 on v6

--- a/solution.py
+++ b/solution.py
@@ -204,7 +204,7 @@
 MESH = pl.DeviceIdType.MESH
 NT = (((1,), (1,)), ((), ()))
 TN = (((0,), (0,)), ((), ()))
-UNROLL = 4
+UNROLL = 8
 
 
 def position():

time: 119 us -> 118 us (level)
  no operation moved by 1% of the time
where the time goes in v7:
time: 118 us
  Pallas kernels  110 us (93%)
  local copies, waits for them, and re-layouts  3.41 us (3%)
  other arithmetic  3.12 us (3%)
    pallas_call x1, Pallas kernels, head_shards(): pl.pallas_call(functools.partial(fused_kernel, devices, half, heads), out...  110 us
    unnamed x6, local copies, waits for them, and re-layouts  2.58 us

profile of v7, /device:TPU:0, one launch (start us, length us, event | category | flops | bytes accessed | tf_op | source)
XLA Modules:
  0.0 117.6 jit_solution(820564587409317992)
XLA Ops:
  0.7 0.7 dynamic-slice_subtract_fusion
  1.4 0.1 copy.10
  1.5 0.1 sub.30
  1.6 0.1 pad_add_fusion
  1.7 0.1 select_reduce_fusion
  1.8 0.6 reshape.80.table
  2.4 110.4 %head_grads.1 = (bf16[2,128,2048]{2,1,0:T(8,128)(2,1)}, bf16[1024,512]{1,0:T(8,128)(2,1)}, bf16[1024,512]{1,0:T(8,128)(2,1)}) custom-call(s32[160]{0:T(256)} %reshape.80.table, bf16[128,2048]{1,0:T(8,128)(2,1)} %query_ref.1, bf16[128,2048]{1,0:T(8,128)(2,1)} %grad_ref.1, bf16[8,128,512]{2,1,0:T(8,128)(2,1)} %bitcast.4, bf16[8,128,512]{2,1,0:T(8,128)(2,1)} %bitcast.5), custom_call_target="tpu_custom_call" | custom-call | tf_op jit(solution)/shard_map/head_grads/pallas_call | solution.py:474
  112.8 0.0 copy-start.1
  112.8 2.2 %fusion = bf16[128,2048]{1,0:T(8,128)(2,1)} fusion(bf16[2,128,2048]{2,1,0:T(8,128)(2,1)} %get-tuple-element.6), kind=kLoop, calls=%fused_computation.1 | loop fusion | flops 1048576 | bytes 1572864 | tf_op jit(solution)/shard_map/convert_element_type | solution.py:513
  115.0 0.0 copy-done.1
  115.0 0.0 copy-start
  115.0 1.0 copy.13
  116.0 0.6 copy-done
  116.7 1.0 copy.14
  (7 shorter events, 0.0 us)
Async XLA Ops:
  112.8 2.2 %copy-start.1 = (bf16[1024,512]{1,0:T(8,128)(2,1)S(1)}, bf16[1024,512]{1,0:T(8,128)(2,1)}, u32[]{:S(2)}) copy-start(bf16[1024,512]{1,0:T(8,128)(2,1)} %get-tuple-element.15) | copy-start | bytes 3145732
  115.0 1.6 %copy-start = (bf16[1024,512]{1,0:T(8,128)(2,1)S(1)}, bf16[1024,512]{1,0:T(8,128)(2,1)}, u32[]{:S(2)}) copy-start(bf16[1024,512]{1,0:T(8,128)(2,1)} %get-tuple-element.16) | copy-start | bytes 3145732
